TPU v7x, 32 devices: a whole 2x2x4 slice. The times are simulated.
32 devices in a mesh: ha: 2 (over x), wa: 16 (over z, y, core).
Axes of the slice: x: 2, y: 2, z: 4, core: 2. Of those that a mesh axis runs over, the one named last changes fastest.
Arguments:
- queries: float32 [2, 16, 128, 256], P(None, 'ha', 'wa'), may hold values from -240 to 240
- keys: float32 [2, 16, 128, 256], P(None, 'ha', 'wa'), may hold values from -6 to 6
- values: float32 [2, 16, 128, 256], P(None, 'ha', 'wa'), may hold values from -6 to 6
- cotangent: float32 [2, 16, 128, 256], P(None, 'ha', 'wa'), may hold values from -6 to 6
Outputs:
- query_grad: float32 [2, 16, 128, 256], P(None, 'ha', 'wa')
- key_grad: float32 [2, 16, 128, 256], P(None, 'ha', 'wa')
- value_grad: float32 [2, 16, 128, 256], P(None, 'ha', 'wa')
All inputs are finite; a program needn't handle non-finite values.
Results may differ from a plain program's by a relative error of at most 0.0003.
Values sent between devices are 32-bit elements; how exact they have to be, the bound alone decides.
No kernel may reach another device: no remote copies, remote signals or barrier semaphores. Data moves between devices by JAX's collectives and lax.ppermute only.
A program may use at most 128 MiB of HBM per device.

v0:
```python
import functools

import jax
import jax.numpy as jnp
from jax import lax
from jax.experimental import pallas as pl
from jax.experimental.pallas import tpu as pltpu
from jax.sharding import PartitionSpec as P

HEADS = 4
REACH = 3
FAR = 1000
NEG = -1e30
BF = jnp.bfloat16
F32 = jnp.float32


def vmem(rows, columns=256, dtype=F32):
    return pltpu.VMEM((rows, columns), dtype)


def held(x):
    return pltpu.with_memory_space_constraint(x, pltpu.VMEM)


def slot_column(p, slot):
    turned = jnp.where(slot < 3, slot + 5, jnp.where(slot < 6, slot - 1, slot - 6))
    return jnp.where(p == 0, slot, turned)


def pack_kernel(q_ref, k_ref, v_ref, c_ref, corner_ref, rest_ref, odd_ref, even_ref,
                own_q_ref, own_k_ref, own_v_ref, own_c_ref, split_ref):
    h = lax.axis_index("ha")
    p = lax.axis_index("wa") % 2
    row_in = jnp.where(h == 0, 5, 0)
    row_out = jnp.where(h == 0, 2, 3)
    even_in = jnp.where(p == 0, 5, 0)
    even_out = jnp.where(p == 0, 2, 3)
    slots = [slot_column(p, slot) for slot in range(8)]

    fields = ((k_ref, own_k_ref, True), (v_ref, own_v_ref, True),
              (q_ref, own_q_ref, False), (c_ref, own_c_ref, False))
    for index, (ref, _, _) in enumerate(fields):
        for half in range(2):
            split_ref[2 * index + half] = ref[:, 128 * half : 128 * half + 128]

    def col(index, image, column, first, count):
        rows = pl.ds(image * 64 + first * 8 + column, count, stride=8)
        return jnp.concatenate([split_ref[2 * index + half, rows, :] for half in range(2)], axis=1)

    for image in range(2):
        at, rest = 90 * image, 54 * image
        for index, (_, _, wide) in enumerate(fields):
            pieces = [(row_in, slot) for slot in range(6 if wide else 3)]
            pieces += [(row_out, slot) for slot in range(6)] if wide else []
            for first, slot in pieces:
                corner_ref[at : at + 3, :] = col(index, image, slots[slot], first, 3)
                at += 3
            pieces = [(row_in, slot) for slot in ((6, 7) if wide else (3, 4, 5, 6, 7))]
            pieces += [(row_out, slot) for slot in (6, 7)] if wide else []
            for first, slot in pieces:
                rest_ref[rest : rest + 3, :] = col(index, image, slots[slot], first, 3)
                rest += 3
    for image in range(2):
        at = 144 * image
        for index, (_, own_ref, wide) in enumerate(fields):
            for slot in range(8):
                x = col(index, image, slots[slot], 0, 8)
                own_ref[64 * image + 8 * slot : 64 * image + 8 * slot + 8, :] = x
                if slot < (6 if wide else 3):
                    odd_ref[at + 8 * slot : at + 8 * slot + 8, :] = x
            for j in range(6 if wide else 3):
                even_ref[at + 8 * j : at + 8 * j + 8, :] = col(
                    index, image, even_in + j if j < 3 else even_out + j - 3, 0, 8
                )
            at += 48 if wide else 24


def third(i):
    return (i * 43) >> 7


class Places:
    def __init__(self, cols):
        h = lax.axis_index("ha")
        w = lax.axis_index("wa")
        self.p = p = w % 2
        lost = jnp.where(jnp.logical_or(w == 0, w == cols - 1), FAR, 0)
        self.row_in = jnp.where(h == 0, 8, -3)
        self.row_out = jnp.where(h == 0, 11, -6)
        self.even_in = jnp.where(p == 0, 8, -3)
        self.even_out = jnp.where(p == 0, 11, -6)
        self.even_all = jnp.where(p == 0, 8, -8)
        self.odd_in = jnp.where(p == 0, -3, 8) + lost
        self.odd_out = jnp.where(p == 0, -6, 11) + lost

    def own(self, i, slot=0):
        return i & 7, slot_column(self.p, slot + (i >> 3))

    def ha_in(self, i, slot=0):
        j = third(i)
        return self.row_in + (i - 3 * j), slot_column(self.p, slot + j)

    def ha_out(self, i):
        j = third(i)
        return self.row_out + (i - 3 * j), slot_column(self.p, j)

    def deven_in(self, i):
        j = third(i)
        return self.row_in + (i - 3 * j), self.even_all + slot_column(1 - self.p, j)

    def deven_out(self, i):
        j = third(i)
        return self.row_out + (i - 3 * j), self.even_all + slot_column(1 - self.p, j)

    def even_inner(self, i):
        return i & 7, self.even_in + (i >> 3)

    def even_outer(self, i):
        return i & 7, self.even_out + (i >> 3)

    def odd_inner(self, i):
        return i & 7, self.odd_in + (i >> 3)

    def odd_outer(self, i):
        return i & 7, self.odd_out + (i >> 3)

    def dodd_in(self, i):
        j = third(i)
        return self.row_in + (i - 3 * j), self.odd_in + j

    def dodd_out(self, i):
        near = i < 9
        k = jnp.where(near, i, i - 9)
        j = third(k)
        row = jnp.where(near, self.row_in, self.row_out) + (k - 3 * j)
        column = jnp.where(
            near, self.odd_out + j, jnp.where(j < 3, self.odd_in + j, self.odd_out + j - 3)
        )
        return row, column


def write_bias(bias_ref, key_segments, token_segments):
    lane = lax.broadcasted_iota(jnp.int32, (8, 128), 1)
    token_r = jnp.full((8, 128), 3 * FAR, jnp.int32)
    token_c = jnp.full((8, 128), 3 * FAR, jnp.int32)
    first = 0
    for place, real, count in token_segments:
        r, c = place(jnp.clip(lane - first, 0, real - 1))
        inside = jnp.logical_and(lane >= first, lane < first + real)
        token_r = jnp.where(inside, r, token_r)
        token_c = jnp.where(inside, c, token_c)
        first += count
    width = bias_ref.shape[1]
    at = 0
    for place, real, count in key_segments:
        for group in range(count // 8):
            i = lax.broadcasted_iota(jnp.int32, (8, 128), 0) + 8 * group
            r, c = place(jnp.minimum(i, real - 1))
            if 8 * group + 8 > real:
                r = jnp.where(i < real, r, -FAR)
            near = jnp.logical_and(jnp.abs(r - token_r) <= REACH, jnp.abs(c - token_c) <= REACH)
            bias_ref[at : at + 8, :] = jnp.where(near, 0.0, NEG).astype(F32)[:, 0:width]
            at += 8


def rounded(x):
    return x.astype(BF).astype(F32)


def halves(x, parts):
    out = []
    for part in range(parts):
        top = rounded(x)
        out.append((top, pltpu.roll(top, 64, 1)))
        if part + 1 < parts:
            x = x - top
    return out


def side(low, a, b, upper):
    if upper:
        return jnp.where(low, b[1], a[0])
    return jnp.where(low, a[0], b[1])


def stacked(x, left, parts):
    low = lax.broadcasted_iota(jnp.int32, (1, 128), 1) < 64
    out = []
    for pair in range(2):
        comps = halves(x[:, 128 * pair : 128 * pair + 128], parts)
        for upper in (False, True):
            if parts == 3:
                hi, mid, lo = comps
                if left:
                    a = side(low, hi, mid, upper).astype(BF)
                    pieces = [a, a, side(low, hi, lo, upper).astype(BF)]
                else:
                    pieces = [
                        side(low, hi, hi, upper).astype(BF),
                        side(low, mid, mid, upper).astype(BF),
                        side(low, lo, hi, upper).astype(BF),
                    ]
            else:
                hi, lo = comps
                if left:
                    a = side(low, hi, lo, upper).astype(BF)
                    pieces = [a, a]
                else:
                    pieces = [
                        side(low, hi, hi, upper).astype(BF),
                        side(low, lo, lo, upper).astype(BF),
                    ]
            out.append(jnp.concatenate(pieces, axis=1))
    return out


def dot_nt(a, b):
    return lax.dot_general(a, b, (((1,), (1,)), ((), ())), preferred_element_type=F32)


def dot_nn(a, b):
    return lax.dot_general(a, b, (((1,), (0,)), ((), ())), preferred_element_type=F32)


def two(x):
    hi = x.astype(BF)
    return hi, (x - hi.astype(F32)).astype(BF)


def heads_product(per_head, field):
    lane_head = lax.broadcasted_iota(jnp.int32, (1, 256), 1) >> 6
    rows = per_head[0].shape[0]
    left_hi, left_lo = two(jnp.concatenate(per_head, axis=0))
    right_hi, right_lo = two(field)
    full = dot_nn(left_hi, right_hi) + (dot_nn(left_lo, right_hi) + dot_nn(left_hi, right_lo))
    out = full[0:rows]
    for head in range(1, HEADS):
        out = jnp.where(lane_head == head, full[rows * head : rows * head + rows], out)
    return out


def attend(key, value, query, cot, bias_ref, own_tokens, own_keys, inner_keys):
    query = query * 0.125
    key_l, value_l = stacked(key, True, 3), stacked(value, True, 2)
    query_r, cot_r = stacked(query, False, 3), stacked(cot, False, 2)
    prob_rows, ds_rows, ds_cols = [], [], []
    for head in range(HEADS):
        s = dot_nt(key_l[head], query_r[head]) + bias_ref[...]
        dp = dot_nt(value_l[head], cot_r[head])
        top = jnp.maximum(jnp.max(s, axis=0, keepdims=True), -1e29)
        e = jnp.exp(s - top)
        inv = 1.0 / jnp.maximum(jnp.sum(e, axis=0, keepdims=True), 1e-30)
        delta = inv * jnp.sum(e * dp, axis=0, keepdims=True)
        probs = e[0:inner_keys] * inv
        ds = probs * (dp[0:inner_keys] - delta)
        prob_rows.append(probs[0:own_keys])
        ds_rows.append(ds[0:own_keys])
        ds_cols.append(ds[:, 0:own_tokens].T)
    return (
        heads_product(ds_cols, key[0:inner_keys]) * 0.125,
        heads_product(ds_rows, query),
        heads_product(prob_rows, cot),
    )


def rows(ref, first, count, pad=0):
    x = ref[first : first + count, :]
    return [x, jnp.zeros((pad, 256), F32)] if pad else [x]


CORNER = (0, 36, 72, 81)
REST = (0, 12, 24, 39)
SIDE = (0, 48, 96, 120)


def even_kernel(cols, own_q_ref, own_k_ref, own_v_ref, own_c_ref, corner_ref, rest_ref, even_ref, mate_corner_ref,
                mate_rest_ref, dq_ref, dk_ref, dv_ref, bias_ref):
    at = Places(cols)
    write_bias(
        bias_ref,
        ((at.own, 64, 64), (at.ha_in, 24, 24), (at.even_inner, 24, 24), (at.deven_in, 24, 24),
         (at.ha_out, 24, 24), (at.even_outer, 24, 24), (at.deven_out, 24, 24)),
        ((lambda i: at.own(i, 3), 40, 40), (lambda i: at.ha_in(i, 3), 15, 16), (at.even_inner, 24, 24),
         (at.deven_in, 24, 24)),
    )
    for image in range(2):

        def keys(own_ref, field):
            corner, rest, even = 90 * image + CORNER[field], 54 * image + REST[field], 144 * image + SIDE[field]
            out = rows(own_ref, 64 * image, 64)
            out += rows(corner_ref, corner, 18) + rows(rest_ref, rest, 6)
            out += rows(even_ref, even, 24)
            out += rows(mate_corner_ref, corner, 18) + rows(mate_rest_ref, rest, 6)
            out += rows(corner_ref, corner + 18, 18) + rows(rest_ref, rest + 6, 6)
            out += rows(even_ref, even + 24, 24)
            out += rows(mate_corner_ref, corner + 18, 18) + rows(mate_rest_ref, rest + 6, 6)
            return jnp.concatenate(out, axis=0)

        def tokens(own_ref, field):
            corner, rest, even = 90 * image + CORNER[field], 54 * image + REST[field], 144 * image + SIDE[field]
            out = rows(own_ref, 64 * image + 24, 40)
            out += rows(rest_ref, rest, 15, 1)
            out += rows(even_ref, even, 24)
            out += rows(mate_corner_ref, corner, 9) + rows(mate_rest_ref, rest, 15)
            return jnp.concatenate(out, axis=0)

        dq, dk, dv = attend(
            keys(own_k_ref, 0), keys(own_v_ref, 1), tokens(own_q_ref, 2), tokens(own_c_ref, 3), bias_ref, 40, 64, 136
        )
        dq_ref[40 * image : 40 * image + 40, :] = dq
        dk_ref[64 * image : 64 * image + 64, :] = dk
        dv_ref[64 * image : 64 * image + 64, :] = dv


def odd_kernel(cols, own_q_ref, own_k_ref, own_v_ref, own_c_ref, corner_ref, odd_ref, far_ref, even_dq_ref, even_dk_ref,
               even_dv_ref, dq_ref, dk_ref, dv_ref, bias_ref, split_ref):
    at = Places(cols)
    write_bias(
        bias_ref,
        ((at.own, 48, 48), (at.ha_in, 18, 24), (at.odd_inner, 24, 24), (at.dodd_in, 9, 16),
         (at.ha_out, 18, 24), (at.odd_outer, 24, 24), (at.dodd_out, 27, 32)),
        ((at.own, 24, 24), (at.ha_in, 9, 16), (at.odd_inner, 24, 24), (at.dodd_in, 9, 16)),
    )
    for image in range(2):

        def keys(own_ref, field):
            corner, odd = 90 * image + CORNER[field], 144 * image + SIDE[field]
            out = rows(own_ref, 64 * image, 48)
            out += rows(corner_ref, corner, 18, 6) + rows(odd_ref, odd, 24) + rows(far_ref, corner, 9, 7)
            out += rows(corner_ref, corner + 18, 18, 6) + rows(odd_ref, odd + 24, 24) + rows(far_ref, corner + 9, 27, 5)
            return jnp.concatenate(out, axis=0)

        def tokens(own_ref, field):
            corner, odd = 90 * image + CORNER[field], 144 * image + SIDE[field]
            out = rows(own_ref, 64 * image, 24)
            out += rows(corner_ref, corner, 9, 7) + rows(odd_ref, odd, 24) + rows(far_ref, corner, 9, 7)
            return jnp.concatenate(out, axis=0)

        dq, dk, dv = attend(
            keys(own_k_ref, 0), keys(own_v_ref, 1), tokens(own_q_ref, 2), tokens(own_c_ref, 3), bias_ref, 24, 48, 112
        )
        here = slice(64 * image, 64 * image + 64)
        none = jnp.zeros((16, 256), F32)
        results = (
            jnp.concatenate([dq, even_dq_ref[40 * image : 40 * image + 40, :]], axis=0),
            jnp.concatenate([dk, none], axis=0) + even_dk_ref[here, :],
            jnp.concatenate([dv, none], axis=0) + even_dv_ref[here, :],
        )
        for index, x in enumerate(results):
            for slot in range(8):
                where = pl.ds(64 * image + slot_column(at.p, slot), 8, stride=8)
                for half in range(2):
                    split_ref[2 * index + half, where, :] = x[8 * slot : 8 * slot + 8, 128 * half : 128 * half + 128]
    for index, ref in enumerate((dq_ref, dk_ref, dv_ref)):
        for half in range(2):
            ref[:, 128 * half : 128 * half + 128] = split_ref[2 * index + half]


def cost(micros):
    return pl.CostEstimate(flops=0, bytes_accessed=int(micros * 3e6), transcendentals=0)


def per_device(queries, keys, values, cotangent):
    shape = queries.shape
    cols = lax.axis_size("wa")
    flat = [x.reshape(128, 256) for x in (queries, keys, values, cotangent)]
    to_corner, to_rest, to_odd, to_even, *own = pl.pallas_call(
        pack_kernel,
        out_shape=(vmem(184), vmem(112), vmem(288), vmem(288)) + (vmem(128),) * 4,
        scratch_shapes=[pltpu.VMEM((8, 128, 128), F32)],
        name="pack",
    )(*flat)

    both = ("ha", "wa")
    ends = (0, cols - 1)
    partner = {i: (i + 1 if i % 2 else i - 1) for i in range(cols) if i not in ends}
    main_pairs, corner_pairs = [], []
    for row in range(2):
        for col in range(cols):
            here = row * cols + col
            if col in ends:
                main_pairs.append((here, row * cols + ends[1 - ends.index(col)]))
                corner_pairs.append((here, (1 - row) * cols + col))
            else:
                main_pairs.append((here, row * cols + partner[col]))
                corner_pairs.append((here, row * cols + partner[col]))
    even_pairs = [(i, i ^ 1) for i in range(cols)]
    across = [(0, 1), (1, 0)]

    corner = lax.ppermute(to_corner, "ha", across)
    odd = lax.ppermute(to_odd, both, main_pairs)
    rest = lax.ppermute(to_rest, "ha", across)
    even = lax.ppermute(to_even, "wa", even_pairs)
    far = lax.ppermute(corner, both, corner_pairs)
    mate_corner = lax.ppermute(corner, "wa", even_pairs)
    mate_rest = lax.ppermute(rest, "wa", even_pairs)

    even_part = pl.pallas_call(
        functools.partial(even_kernel, cols),
        out_shape=(vmem(80), vmem(128), vmem(128)),
        scratch_shapes=[pltpu.VMEM((208, 104), F32)],
        compiler_params=pltpu.CompilerParams(vmem_limit_bytes=32 * 1024 * 1024),
        name="even_set",
    )(*[held(x) for x in (*own, corner, rest, even, mate_corner, mate_rest)])
    out = jax.ShapeDtypeStruct((128, 256), F32)
    grads = pl.pallas_call(
        functools.partial(odd_kernel, cols),
        out_shape=(out, out, out),
        scratch_shapes=[pltpu.VMEM((192, 80), F32), pltpu.VMEM((6, 128, 128), F32)],
        compiler_params=pltpu.CompilerParams(vmem_limit_bytes=32 * 1024 * 1024),
        name="odd_set",
    )(*[held(x) for x in (*own, corner, odd, far, *even_part)])
    return tuple(g.reshape(shape) for g in grads)


def solution(mesh):
    spec = P(None, "ha", "wa", None)
    return jax.shard_map(
        per_device,
        mesh=mesh,
        in_specs=(spec,) * 4,
        out_specs=(spec,) * 3,
        check_vma=False,
    )
```

profile of v0, /device:TPU:0, one launch (start us, length us, event | category | flops | bytes accessed | tf_op | source)
XLA Modules:
  0.0 20.4 jit_solution(2378786568831834899)
XLA Ops:
  0.6 1.4 %pack.1 = (f32[184,256]{1,0:T(8,128)S(1)}, f32[112,256]{1,0:T(8,128)S(1)}, f32[288,256]{1,0:T(8,128)S(1)}, f32[288,256]{1,0:T(8,128)S(1)}, f32[128,256]{1,0:T(8,...) custom-call(f32[128,256]{1,0:T(8,128)} %bitcast.7, f32[128,256]{1,0:T(8,128)} %bitcast.8, ...), custom_call_target="tpu_custom_call" | custom-call | tf_op jit(solution)/shard_map/pack/pallas_call | solution.py:368
  2.1 3.0 %collective-permute-start = (f32[184,256]{1,0:T(8,128)S(1)}, f32[184,256]{1,0:T(8,128)S(1)}, u32[]{:S(2)}, u32[]{:S(2)}) collective-permute-start(f32[184,256]{1,0:T(8,128)S(1)} %get-tuple-element.21), channel_id=1, source_target_pairs={{0,16},{16,0},{1,17},{17,1},{2,18},{18,2},{3,19},{19,3},{4,20},{20... | collective-permute-start | bytes 565256 | tf_op jit(solution)/shard_map/ppermute | solution.py:391
  5.1 0.0 collective-permute-start.4
  5.1 4.7 %collective-permute-start.1 = (f32[288,256]{1,0:T(8,128)S(1)}, f32[288,256]{1,0:T(8,128)S(1)}, u32[]{:S(2)}, u32[]{:S(2)}) collective-permute-start(f32[288,256]{1,0:T(8,128)S(1)} %get-tuple-element.22), channel_id=1, source_target_pairs={{0,15},{1,2},{2,1},{3,4},{4,3},{5,6},{6,5},{7,8},{8,7},{9,10},{10,... | collective-permute-start | bytes 884744 | tf_op jit(solution)/shard_map/ppermute | solution.py:392
  9.7 0.5 %collective-permute-start.3 = (f32[112,256]{1,0:T(8,128)S(1)}, f32[112,256]{1,0:T(8,128)S(1)}, u32[]{:S(2)}, u32[]{:S(2)}) collective-permute-start(f32[112,256]{1,0:T(8,128)S(1)} %get-tuple-element.23), channel_id=1, source_target_pairs={{0,16},{16,0},{1,17},{17,1},{2,18},{18,2},{3,19},{19,3},{4,20},{20... | collective-permute-start | bytes 344072 | tf_op jit(solution)/shard_map/ppermute | solution.py:393
  10.3 0.0 collective-permute-done.corner_ref
  10.3 0.0 collective-permute-start.5
  10.3 2.4 %collective-permute-start.2 = (f32[184,256]{1,0:T(8,128)S(1)}, f32[184,256]{1,0:T(8,128)S(1)}, u32[]{:S(2)}, u32[]{:S(2)}) collective-permute-start(f32[184,256]{1,0:T(8,128)S(1)} %collective-permute-done.corner_ref), channel_id=1, source_target_pairs={{0,16},{1,2},{2,1},{3,4},{4,3},{5,6},{6,5},{7,8},{8,7},{9,10},{10,... | collective-permute-start | bytes 565256 | tf_op jit(solution)/shard_map/ppermute | solution.py:395
  12.7 1.8 %collective-permute-done.3.rest_ref = f32[112,256]{1,0:T(8,128)S(1)} collective-permute-done((f32[112,256]{1,0:T(8,128)S(1)}, f32[112,256]{1,0:T(8,128)S(1)}, u32[]{:S(2)}, u32[]{:S(2)}) %collective-permute-start.3) | collective-permute-done | bytes 114720 | tf_op jit(solution)/shard_map/ppermute | solution.py:393
  14.5 0.0 collective-permute-start.6
  14.5 1.3 %collective-permute-done.6.mate_rest_ref = f32[112,256]{1,0:T(8,128)S(1)} collective-permute-done((f32[112,256]{1,0:T(8,128)S(1)}, f32[112,256]{1,0:T(8,128)S(1)}, u32[]{:S(2)}, u32[]{:S(2)}) %collective-permute-start.6) | collective-permute-done | bytes 114720 | tf_op jit(solution)/shard_map/ppermute | solution.py:397
  15.9 0.0 collective-permute-done.4.even_ref
  15.9 0.0 collective-permute-done.5.mate_corner_ref
  15.9 2.1 %even_set.1 = (f32[80,256]{1,0:T(8,128)S(1)}, f32[128,256]{1,0:T(8,128)S(1)}, f32[128,256]{1,0:T(8,128)S(1)}) custom-call(f32[128,256]{1,0:T(8,128)S(1)} %get-tuple-element.17.own_q_ref, f32[128,256]{1,0:T(8,128)S(1)} %get-tuple-element.18.own_k_ref, f32[128,256]{1,0:T(8,128)S(1)} %get-tuple-element.19.own_v_ref, ...), custom_call_target="tpu_custom_call" | custom-call | tf_op jit(solution)/shard_map/even_set/pallas_call | solution.py:399
  18.0 0.0 collective-permute-done.1.odd_ref
  18.0 0.0 collective-permute-done.2.far_ref
  18.0 2.4 %odd_set.1 = (f32[128,256]{1,0:T(8,128)}, f32[128,256]{1,0:T(8,128)}, f32[128,256]{1,0:T(8,128)}) custom-call(f32[128,256]{1,0:T(8,128)S(1)} %get-tuple-element.17.own_q_ref, f32[128,256]{1,0:T(8,128)S(1)} %get-tuple-element.18.own_k_ref, f32[128,256]{1,0:T(8,128)S(1)} %get-tuple-element.19.own_v_ref, f32[128,256]{1,0:T(8,128)S(1)} %get-tuple-element.20.own_c_ref, ...), custom_call_target="tpu_custom_call" | custom-call | tf_op jit(solution)/shard_map/odd_set/pallas_call | solution.py:407
Async XLA Ops:
  2.1 8.2 %collective-permute-start = (f32[184,256]{1,0:T(8,128)S(1)}, f32[184,256]{1,0:T(8,128)S(1)}, u32[]{:S(2)}, u32[]{:S(2)}) collective-permute-start(f32[184,256]{1,0:T(8,128)S(1)} %get-tuple-element.21), channel_id=1, source_target_pairs={{0,16},{16,0},{1,17},{17,1},{2,18},{18,2},{3,19},{19,3},{4,20},{20... | collective-permute-start | bytes 565256 | tf_op jit(solution)/shard_map/ppermute | solution.py:391
  5.1 10.8 %collective-permute-start.4 = (f32[288,256]{1,0:T(8,128)S(1)}, f32[288,256]{1,0:T(8,128)S(1)}, u32[]{:S(2)}, u32[]{:S(2)}) collective-permute-start(f32[288,256]{1,0:T(8,128)S(1)} %get-tuple-element.24), channel_id=1, source_target_pairs={{0,1},{1,0},{2,3},{3,2},{4,5},{5,4},{6,7},{7,6},{8,9},{9,8},{10,11... | collective-permute-start | bytes 884744 | tf_op jit(solution)/shard_map/ppermute | solution.py:394
  5.1 12.9 %collective-permute-start.1 = (f32[288,256]{1,0:T(8,128)S(1)}, f32[288,256]{1,0:T(8,128)S(1)}, u32[]{:S(2)}, u32[]{:S(2)}) collective-permute-start(f32[288,256]{1,0:T(8,128)S(1)} %get-tuple-element.22), channel_id=1, source_target_pairs={{0,15},{1,2},{2,1},{3,4},{4,3},{5,6},{6,5},{7,8},{8,7},{9,10},{10,... | collective-permute-start | bytes 884744 | tf_op jit(solution)/shard_map/ppermute | solution.py:392
  9.7 4.8 %collective-permute-start.3 = (f32[112,256]{1,0:T(8,128)S(1)}, f32[112,256]{1,0:T(8,128)S(1)}, u32[]{:S(2)}, u32[]{:S(2)}) collective-permute-start(f32[112,256]{1,0:T(8,128)S(1)} %get-tuple-element.23), channel_id=1, source_target_pairs={{0,16},{16,0},{1,17},{17,1},{2,18},{18,2},{3,19},{19,3},{4,20},{20... | collective-permute-start | bytes 344072 | tf_op jit(solution)/shard_map/ppermute | solution.py:393
  10.3 5.6 %collective-permute-start.5 = (f32[184,256]{1,0:T(8,128)S(1)}, f32[184,256]{1,0:T(8,128)S(1)}, u32[]{:S(2)}, u32[]{:S(2)}) collective-permute-start(f32[184,256]{1,0:T(8,128)S(1)} %collective-permute-done.corner_ref), channel_id=1, source_target_pairs={{0,1},{1,0},{2,3},{3,2},{4,5},{5,4},{6,7},{7,6},{8,9},{9,8},{10,11... | collective-permute-start | bytes 565256 | tf_op jit(solution)/shard_map/ppermute | solution.py:396
  10.3 7.7 %collective-permute-start.2 = (f32[184,256]{1,0:T(8,128)S(1)}, f32[184,256]{1,0:T(8,128)S(1)}, u32[]{:S(2)}, u32[]{:S(2)}) collective-permute-start(f32[184,256]{1,0:T(8,128)S(1)} %collective-permute-done.corner_ref), channel_id=1, source_target_pairs={{0,16},{1,2},{2,1},{3,4},{4,3},{5,6},{6,5},{7,8},{8,7},{9,10},{10,... | collective-permute-start | bytes 565256 | tf_op jit(solution)/shard_map/ppermute | solution.py:395
  14.5 1.3 %collective-permute-start.6 = (f32[112,256]{1,0:T(8,128)S(1)}, f32[112,256]{1,0:T(8,128)S(1)}, u32[]{:S(2)}, u32[]{:S(2)}) collective-permute-start(f32[112,256]{1,0:T(8,128)S(1)} %collective-permute-done.3.rest_ref), channel_id=1, source_target_pairs={{0,1},{1,0},{2,3},{3,2},{4,5},{5,4},{6,7},{7,6},{8,9},{9,8},{10,11... | collective-permute-start | bytes 344072 | tf_op jit(solution)/shard_map/ppermute | solution.py:397
where the time goes:
time: 20.6 us; the launch traced here: 20.4 us
  starting transfers between devices  10.6 us (51%)
  Pallas kernels  5.96 us (29%)
  waiting for transfers between devices  3.18 us (15%)
  between operations  0.66 us (3%)
    ppermute x1, starting transfers between devices, per_device(): odd = lax.ppermute(to_odd, both, main_pairs)  4.67 us
    ppermute x1, starting transfers between devices, per_device(): corner = lax.ppermute(to_corner, 'ha', across)  3 us
    pallas_call x1, Pallas kernels, per_device(): pl.pallas_call(functools.partial(odd_kernel, cols), out_shape=(out, out,...  2.43 us
    ppermute x1, starting transfers between devices, per_device(): far = lax.ppermute(corner, both, corner_pairs)  2.4 us
    pallas_call x1, Pallas kernels, per_device(): pl.pallas_call(functools.partial(even_kernel, cols), out_shape=(vmem(80),...  2.11 us
    ppermute x1, waiting for transfers between devices, per_device(): rest = lax.ppermute(to_rest, 'ha', across)  1.85 us
    pallas_call x1, Pallas kernels, per_device(): pl.pallas_call(pack_kernel, out_shape=(vmem(184), vmem(112), vmem(288), v...  1.42 us
    ppermute x1, waiting for transfers between devices, per_device(): mate_rest = lax.ppermute(rest, 'wa', even_pairs)  1.32 us
  transfers between devices with their start and end apart: 7, of which 2 were waited for; matrix products, arithmetic and copies ran while one was open for 0% of the time, Pallas kernels for 10%

commit v1 on v0

v1 whole, which is shorter than its diff:
```python
import functools

import jax
import jax.numpy as jnp
from jax import lax
from jax.experimental import pallas as pl
from jax.experimental.pallas import tpu as pltpu
from jax.sharding import PartitionSpec as P

HEADS = 4
REACH = 3
FAR = 1000
NEG = -1e30
BF = jnp.bfloat16
F32 = jnp.float32


def vmem(rows, columns=256, dtype=F32):
    return pltpu.VMEM((rows, columns), dtype)


def held(x):
    return pltpu.with_memory_space_constraint(x, pltpu.VMEM)


def slot_column(p, slot):
    turned = jnp.where(slot < 3, slot + 5, jnp.where(slot < 6, slot - 1, slot - 6))
    return jnp.where(p == 0, slot, turned)


def pack_reader(split_ref):
    def col(index, image, column, first, count):
        rows = pl.ds(image * 64 + first * 8 + column, count, stride=8)
        return jnp.concatenate([split_ref[2 * index + half, rows, :] for half in range(2)], axis=1)

    return col


WIDE = (True, True, False, False)


def corner_kernel(k_ref, v_ref, q_ref, c_ref, corner_ref, split_ref):
    h = lax.axis_index("ha")
    p = lax.axis_index("wa") % 2
    row_in = jnp.where(h == 0, 5, 0)
    row_out = jnp.where(h == 0, 2, 3)
    col = pack_reader(split_ref)
    for index, ref in enumerate((k_ref, v_ref, q_ref, c_ref)):
        for half in range(2):
            split_ref[2 * index + half] = ref[:, 128 * half : 128 * half + 128]
    for image in range(2):
        at = 90 * image
        for index, wide in enumerate(WIDE):
            pieces = [(row_in, slot) for slot in range(6 if wide else 3)]
            pieces += [(row_out, slot) for slot in range(6)] if wide else []
            for first, slot in pieces:
                corner_ref[at : at + 3, :] = col(index, image, slot_column(p, slot), first, 3)
                at += 3


def pack_kernel(split_ref, rest_ref, odd_rest_ref, even_ref, own_k_ref, own_v_ref, own_q_ref, own_c_ref):
    h = lax.axis_index("ha")
    p = lax.axis_index("wa") % 2
    row_in = jnp.where(h == 0, 5, 0)
    row_out = jnp.where(h == 0, 2, 3)
    row_far = jnp.where(h == 0, 0, 6)
    row_rest = jnp.where(h == 0, 0, 3)
    even_in = jnp.where(p == 0, 5, 0)
    even_out = jnp.where(p == 0, 2, 3)
    slots = [slot_column(p, slot) for slot in range(8)]
    col = pack_reader(split_ref)
    for image in range(2):
        rest, odd_rest = 54 * image, 54 * image
        for index, wide in enumerate(WIDE):
            pieces = [(row_in, slot) for slot in ((6, 7) if wide else (3, 4, 5, 6, 7))]
            pieces += [(row_out, slot) for slot in (6, 7)] if wide else []
            for first, slot in pieces:
                rest_ref[rest : rest + 3, :] = col(index, image, slots[slot], first, 3)
                rest += 3
            for slot in range(6 if wide else 3):
                first, count = (row_far, 2) if wide else (row_rest, 5)
                odd_rest_ref[odd_rest : odd_rest + count, :] = col(index, image, slots[slot], first, count)
                odd_rest += count
    for image in range(2):
        at = 144 * image
        for index, (own_ref, wide) in enumerate(zip((own_k_ref, own_v_ref, own_q_ref, own_c_ref), WIDE)):
            for slot in range(8):
                own_ref[64 * image + 8 * slot : 64 * image + 8 * slot + 8, :] = col(index, image, slots[slot], 0, 8)
            for j in range(6 if wide else 3):
                even_ref[at + 8 * j : at + 8 * j + 8, :] = col(
                    index, image, even_in + j if j < 3 else even_out + j - 3, 0, 8
                )
            at += 48 if wide else 24


def third(i):
    return (i * 43) >> 7


class Places:
    def __init__(self, cols):
        h = lax.axis_index("ha")
        w = lax.axis_index("wa")
        self.p = p = w % 2
        lost = jnp.where(jnp.logical_or(w == 0, w == cols - 1), FAR, 0)
        self.row_in = jnp.where(h == 0, 8, -3)
        self.row_out = jnp.where(h == 0, 11, -6)
        self.even_in = jnp.where(p == 0, 8, -3)
        self.even_out = jnp.where(p == 0, 11, -6)
        self.even_all = jnp.where(p == 0, 8, -8)
        self.row_near = jnp.where(h == 0, 5, 0)
        self.row_next = jnp.where(h == 0, 2, 3)
        self.row_far = jnp.where(h == 0, 0, 6)
        self.row_rest = jnp.where(h == 0, 0, 3)
        self.odd_in = jnp.where(p == 0, -3, 8) + lost
        self.odd_out = jnp.where(p == 0, -6, 11) + lost

    def own(self, i, slot=0):
        return i & 7, slot_column(self.p, slot + (i >> 3))

    def ha_in(self, i, slot=0):
        j = third(i)
        return self.row_in + (i - 3 * j), slot_column(self.p, slot + j)

    def ha_out(self, i):
        j = third(i)
        return self.row_out + (i - 3 * j), slot_column(self.p, j)

    def deven_in(self, i):
        j = third(i)
        return self.row_in + (i - 3 * j), self.even_all + slot_column(1 - self.p, j)

    def deven_out(self, i):
        j = third(i)
        return self.row_out + (i - 3 * j), self.even_all + slot_column(1 - self.p, j)

    def even_inner(self, i):
        return i & 7, self.even_in + (i >> 3)

    def even_outer(self, i):
        return i & 7, self.even_out + (i >> 3)

    def odd_keys(self, i):
        k = jnp.where(i < 9, i, jnp.where(i < 18, i - 9, 0))
        j = third(k)
        row = jnp.where(i < 9, self.row_near, self.row_next) + (k - 3 * j)
        m = jnp.maximum(i - 18, 0)
        last = i >= 18
        return jnp.where(last, self.row_far + (m & 1), row), jnp.where(last, m >> 1, j)

    def odd_inner(self, i):
        row, j = self.odd_keys(i)
        return row, self.odd_in + j

    def odd_outer(self, i):
        row, j = self.odd_keys(i)
        return row, self.odd_out + j

    def odd_tokens(self, i):
        j = third(i)
        m = jnp.maximum(i - 9, 0)
        fifth = (m * 13) >> 6
        near = i < 9
        return (
            jnp.where(near, self.row_near + (i - 3 * j), self.row_rest + (m - 5 * fifth)),
            self.odd_in + jnp.where(near, j, fifth),
        )

    def dodd_in(self, i):
        j = third(i)
        return self.row_in + (i - 3 * j), self.odd_in + j

    def dodd_out(self, i):
        near = i < 9
        k = jnp.where(near, i, i - 9)
        j = third(k)
        row = jnp.where(near, self.row_in, self.row_out) + (k - 3 * j)
        column = jnp.where(
            near, self.odd_out + j, jnp.where(j < 3, self.odd_in + j, self.odd_out + j - 3)
        )
        return row, column


def write_bias(bias_ref, key_segments, token_segments):
    lane = lax.broadcasted_iota(jnp.int32, (8, 128), 1)
    token_r = jnp.full((8, 128), 3 * FAR, jnp.int32)
    token_c = jnp.full((8, 128), 3 * FAR, jnp.int32)
    first = 0
    for place, real, count in token_segments:
        r, c = place(jnp.clip(lane - first, 0, real - 1))
        inside = jnp.logical_and(lane >= first, lane < first + real)
        token_r = jnp.where(inside, r, token_r)
        token_c = jnp.where(inside, c, token_c)
        first += count
    width = bias_ref.shape[1]
    at = 0
    for place, real, count in key_segments:
        for group in range(count // 8):
            i = lax.broadcasted_iota(jnp.int32, (8, 128), 0) + 8 * group
            r, c = place(jnp.minimum(i, real - 1))
            if 8 * group + 8 > real:
                r = jnp.where(i < real, r, -FAR)
            near = jnp.logical_and(jnp.abs(r - token_r) <= REACH, jnp.abs(c - token_c) <= REACH)
            bias_ref[at : at + 8, :] = jnp.where(near, 0.0, NEG).astype(F32)[:, 0:width]
            at += 8


def rounded(x):
    return x.astype(BF).astype(F32)


def halves(x, parts):
    out = []
    for part in range(parts):
        top = rounded(x)
        out.append((top, pltpu.roll(top, 64, 1)))
        if part + 1 < parts:
            x = x - top
    return out


def side(low, a, b, upper):
    if upper:
        return jnp.where(low, b[1], a[0])
    return jnp.where(low, a[0], b[1])


def stacked(x, left, parts):
    low = lax.broadcasted_iota(jnp.int32, (1, 128), 1) < 64
    out = []
    for pair in range(2):
        comps = halves(x[:, 128 * pair : 128 * pair + 128], parts)
        for upper in (False, True):
            if parts == 3:
                hi, mid, lo = comps
                if left:
                    a = side(low, hi, mid, upper).astype(BF)
                    pieces = [a, a, side(low, hi, lo, upper).astype(BF)]
                else:
                    pieces = [
                        side(low, hi, hi, upper).astype(BF),
                        side(low, mid, mid, upper).astype(BF),
                        side(low, lo, hi, upper).astype(BF),
                    ]
            else:
                hi, lo = comps
                if left:
                    a = side(low, hi, lo, upper).astype(BF)
                    pieces = [a, a]
                else:
                    pieces = [
                        side(low, hi, hi, upper).astype(BF),
                        side(low, lo, lo, upper).astype(BF),
                    ]
            whole = jnp.concatenate(pieces, axis=1)
            if not left:
                whole = jnp.concatenate([whole, jnp.zeros((128 - whole.shape[0], whole.shape[1]), BF)], axis=0)
            out.append(whole)
    return out


def dot_nt(a, b):
    return lax.dot_general(a, b, (((1,), (1,)), ((), ())), preferred_element_type=F32)


def dot_nn(a, b):
    return lax.dot_general(a, b, (((1,), (0,)), ((), ())), preferred_element_type=F32)


def two(x):
    hi = x.astype(BF)
    return hi, (x - hi.astype(F32)).astype(BF)


def heads_product(per_head, field):
    low = lax.broadcasted_iota(jnp.int32, (1, 128), 1) < 64
    rows, depth = per_head[0].shape
    hi, lo = two(field)
    if hi.shape[0] < depth:
        more = jnp.zeros((depth - hi.shape[0], 256), BF)
        hi, lo = jnp.concatenate([hi, more], axis=0), jnp.concatenate([lo, more], axis=0)
    out = []
    for pair in range(2):
        lanes = slice(128 * pair, 128 * pair + 128)
        left_hi, left_lo = two(jnp.concatenate(per_head[2 * pair : 2 * pair + 2], axis=0))
        both = jnp.concatenate([hi[:, lanes], lo[:, lanes]], axis=1)
        if depth == 128:
            below = jnp.concatenate([hi[:, lanes], jnp.zeros((depth, 128), BF)], axis=1)
            full = dot_nn(jnp.concatenate([left_hi, left_lo], axis=1), jnp.concatenate([both, below], axis=0))
            full = full[:, 0:128] + full[:, 128:256]
        else:
            full = dot_nn(left_hi, both)
            full = full[:, 0:128] + (full[:, 128:256] + dot_nn(left_lo, hi[:, lanes]))
        out.append(jnp.where(low, full[0:rows], full[rows : 2 * rows]))
    return jnp.concatenate(out, axis=1)


def attend(work, bias_ref, own_tokens, own_keys, inner):
    scores, dprobs = [], []
    for key_l, value_l, query_r, cot_r, _, _, _ in work:
        for head in range(HEADS):
            scores.append(dot_nt(key_l[head], query_r[head]) + bias_ref[...])
            dprobs.append(dot_nt(value_l[head], cot_r[head]))
    prob_rows, ds_rows, ds_cols = [], [], []
    for s, dp in zip(scores, dprobs):
        top = jnp.maximum(jnp.max(s, axis=0, keepdims=True), -1e29)
        e = jnp.exp(s - top)
        inv = 1.0 / jnp.maximum(jnp.sum(e, axis=0, keepdims=True), 1e-30)
        delta = inv * jnp.sum(e * dp, axis=0, keepdims=True)
        prob_rows.append(e[0:own_keys] * inv)
        ds = [e[part] * inv * (dp[part] - delta) for part in inner]
        ds_rows.append(ds[0][0:own_keys])
        ds = jnp.concatenate(ds, axis=0) if len(ds) > 1 else ds[0]
        ds_cols.append(ds[:, 0:own_tokens].T)
    out = []
    for image, (_, _, _, _, key, query, cot) in enumerate(work):
        here = slice(HEADS * image, HEADS * image + HEADS)
        out.append((
            heads_product(ds_cols[here], key) * 0.125,
            heads_product(ds_rows[here], query),
            heads_product(prob_rows[here], cot),
        ))
    return out


def rows(ref, first, count, pad=0):
    x = ref[first : first + count, :]
    return [x, jnp.zeros((pad, 256), F32)] if pad else [x]


CORNER = (0, 36, 72, 81)
REST = (0, 12, 24, 39)
SIDE = (0, 48, 96, 120)


def even_kernel(cols, own_q_ref, own_k_ref, own_v_ref, own_c_ref, corner_ref, rest_ref, even_ref, mate_ref, dq_ref, dk_ref, dv_ref, bias_ref):
    at = Places(cols)
    write_bias(
        bias_ref,
        ((at.own, 64, 64), (at.ha_in, 24, 24), (at.even_inner, 24, 24), (at.deven_in, 24, 24),
         (at.ha_out, 24, 24), (at.even_outer, 24, 24), (at.deven_out, 24, 24)),
        ((lambda i: at.own(i, 3), 40, 40), (lambda i: at.ha_in(i, 3), 15, 16), (at.even_inner, 24, 24),
         (at.deven_in, 24, 24)),
    )
    work = []
    for image in range(2):

        def keys(own_ref, field):
            corner, rest, even = 90 * image + CORNER[field], 54 * image + REST[field], 144 * image + SIDE[field]
            out = rows(own_ref, 64 * image, 64)
            out += rows(corner_ref, corner, 18) + rows(rest_ref, rest, 6)
            out += rows(even_ref, even, 24)
            out += rows(mate_ref, corner, 18) + rows(mate_ref, 184 + rest, 6)
            out += rows(corner_ref, corner + 18, 18) + rows(rest_ref, rest + 6, 6)
            out += rows(even_ref, even + 24, 24)
            out += rows(mate_ref, corner + 18, 18) + rows(mate_ref, 184 + rest + 6, 6)
            return jnp.concatenate(out, axis=0)

        def tokens(own_ref, field):
            corner, rest, even = 90 * image + CORNER[field], 54 * image + REST[field], 144 * image + SIDE[field]
            out = rows(own_ref, 64 * image + 24, 40)
            out += rows(rest_ref, rest, 15, 1)
            out += rows(even_ref, even, 24)
            out += rows(mate_ref, corner, 9) + rows(mate_ref, 184 + rest, 15, 8)
            return jnp.concatenate(out, axis=0)

        key, query, cot = keys(own_k_ref, 0), tokens(own_q_ref, 2) * 0.125, tokens(own_c_ref, 3)
        work.append((
            stacked(key, True, 3), stacked(keys(own_v_ref, 1), True, 2), stacked(query, False, 3), stacked(cot, False, 2),
            key[0:136], query, cot,
        ))
    for image, (dq, dk, dv) in enumerate(attend(work, bias_ref, 40, 64, (slice(0, 136),))):
        dq_ref[40 * image : 40 * image + 40, :] = dq
        dk_ref[64 * image : 64 * image + 64, :] = dk
        dv_ref[64 * image : 64 * image + 64, :] = dv


def early_tokens(image, own_ref, corner_ref, odd_ref, odd_rest_ref, field):
    corner, rest = 90 * image + CORNER[field], 54 * image + REST[field]
    out = rows(own_ref, 64 * image, 24)
    out += rows(corner_ref, corner, 9, 7)
    out += rows(odd_ref, corner, 9) + rows(odd_rest_ref, rest, 15)
    return jnp.concatenate(out, axis=0)


def sort_kernel(cols, first_ref, second_ref, rest_ref, ha_ref, odd_ref, mate_ref):
    turned = by_row(lax.axis_index("wa"), cols)
    first, second = first_ref[...], second_ref[...]
    ha = jnp.where(turned, second, first)
    ha_ref[...] = ha
    odd_ref[...] = jnp.where(turned, first, second)
    mate_ref[0:184, :] = ha
    mate_ref[184:296, :] = rest_ref[...]


def release_kernel(message_ref, gate_ref, out_ref):
    out_ref[...] = message_ref[...]


def by_row(w, cols):
    return jnp.logical_and(((w + 1) >> 1) % 2 == 0, jnp.logical_and(w > 0, w < cols - 1))


def odd_kernel(cols, own_q_ref, own_k_ref, own_v_ref, own_c_ref, corner_ref, odd_ref, odd_rest_ref, far_ref, even_dq_ref,
               even_dk_ref, even_dv_ref, dq_ref, dk_ref, dv_ref, bias_ref, split_ref):
    at = Places(cols)
    p = at.p
    write_bias(
        bias_ref,
        ((at.own, 48, 48), (at.ha_in, 18, 24), (at.odd_inner, 24, 24), (at.ha_out, 18, 24), (at.odd_outer, 24, 24),
         (at.dodd_in, 9, 16), (at.dodd_out, 27, 32)),
        ((at.own, 24, 24), (at.ha_in, 9, 16), (at.odd_tokens, 24, 24), (at.dodd_in, 9, 16)),
    )
    work = []
    for image in range(2):

        def keys(own_ref, field):
            corner, rest = 90 * image + CORNER[field], 54 * image + REST[field]
            out = rows(own_ref, 64 * image, 48)
            out += rows(corner_ref, corner, 18, 6)
            out += rows(odd_ref, corner, 9) + rows(odd_ref, corner + 18, 9) + rows(odd_rest_ref, rest, 6)
            out += rows(corner_ref, corner + 18, 18, 6)
            out += rows(odd_ref, corner + 9, 9) + rows(odd_ref, corner + 27, 9) + rows(odd_rest_ref, rest + 6, 6)
            out += rows(far_ref, corner, 9, 7) + rows(far_ref, corner + 9, 27, 5)
            return jnp.concatenate(out, axis=0)

        def tokens(own_ref, field):
            corner, rest = 90 * image + CORNER[field], 54 * image + REST[field]
            out = rows(own_ref, 64 * image, 24)
            out += rows(corner_ref, corner, 9, 7)
            out += rows(odd_ref, corner, 9) + rows(odd_rest_ref, rest, 15)
            out += rows(far_ref, corner, 9, 7)
            return jnp.concatenate(out, axis=0)

        key, query, cot = keys(own_k_ref, 0), tokens(own_q_ref, 2) * 0.125, tokens(own_c_ref, 3)
        work.append((
            stacked(key, True, 3), stacked(keys(own_v_ref, 1), True, 2), stacked(query, False, 3), stacked(cot, False, 2),
            jnp.concatenate([key[0:96], key[144:160]], axis=0), query, cot,
        ))
    parts = attend(work, bias_ref, 24, 48, (slice(0, 96), slice(144, 160)))
    for image, (dq, dk, dv) in enumerate(parts):
        here = slice(64 * image, 64 * image + 64)
        none = jnp.zeros((16, 256), F32)
        results = (
            jnp.concatenate([dq, even_dq_ref[40 * image : 40 * image + 40, :]], axis=0),
            jnp.concatenate([dk, none], axis=0) + even_dk_ref[here, :],
            jnp.concatenate([dv, none], axis=0) + even_dv_ref[here, :],
        )
        for index, x in enumerate(results):
            for slot in range(8):
                where = pl.ds(64 * image + slot_column(p, slot), 8, stride=8)
                for half in range(2):
                    split_ref[2 * index + half, where, :] = x[8 * slot : 8 * slot + 8, 128 * half : 128 * half + 128]
    for index, ref in enumerate((dq_ref, dk_ref, dv_ref)):
        for half in range(2):
            ref[:, 128 * half : 128 * half + 128] = split_ref[2 * index + half]


PREP_US = 1
FAR_US = 2
EVEN_US = 0


def cost(micros):
    return pl.CostEstimate(flops=int(micros * 1e9), bytes_accessed=int(micros * 3e6), transcendentals=0)


def per_device(queries, keys, values, cotangent):
    shape = queries.shape
    cols = lax.axis_size("wa")
    flat = [x.reshape(128, 256) for x in (queries, keys, values, cotangent)]
    to_corner, split = pl.pallas_call(
        corner_kernel, out_shape=(vmem(184), pltpu.VMEM((8, 128, 128), F32)), name="corner"
    )(flat[1], flat[2], flat[0], flat[3])
    to_rest, to_odd_rest, to_even, own_k, own_v, own_q, own_c = pl.pallas_call(
        pack_kernel, out_shape=(vmem(112), vmem(112), vmem(288)) + (vmem(128),) * 4, name="pack"
    )(held(split))
    own = (own_q, own_k, own_v, own_c)

    both = ("ha", "wa")
    ends = (0, cols - 1)
    partner = {i: (i + 1 if i % 2 else i - 1) for i in range(cols) if i not in ends}
    first_pairs, second_pairs, far_pairs, odd_pairs = [], [], [], []
    for row in range(2):
        for col in range(cols):
            here, mate = row * cols + col, (1 - row) * cols + col
            beside = mate if col in ends else row * cols + partner[col]
            turned = (col + 1) // 2 % 2 == 0
            first_pairs.append((here, beside if turned else mate))
            far_pairs.append((here, mate if turned else beside))
            second_pairs.append((here, here if col in ends else mate if turned else beside))
            odd_pairs.append((here, beside))
    even_pairs = [(i, i ^ 1) for i in range(cols)]
    across = [(0, 1), (1, 0)]

    first = lax.ppermute(to_corner, both, first_pairs)
    second = lax.ppermute(to_corner, both, second_pairs)
    rest = lax.ppermute(to_rest, "ha", across)
    odd_rest = lax.ppermute(to_odd_rest, both, odd_pairs)
    to_even = pl.pallas_call(release_kernel, out_shape=vmem(288), name="release")(held(to_even), held(first))
    even = lax.ppermute(to_even, "wa", even_pairs)
    far = lax.ppermute(first, both, far_pairs)
    corner, odd, to_mate = pl.pallas_call(
        functools.partial(sort_kernel, cols), out_shape=(vmem(184), vmem(184), vmem(296)), name="sort"
    )(*[held(x) for x in (first, second, rest)])
    mate = lax.ppermute(to_mate, "wa", even_pairs)

    if PREP_US:
        odd_rest = pl.pallas_call(
            release_kernel, out_shape=vmem(112), cost_estimate=cost(PREP_US), name="arrive"
        )(held(odd_rest), held(first))
    if FAR_US:
        far = pl.pallas_call(
            release_kernel, out_shape=vmem(184), cost_estimate=cost(FAR_US), name="arrive_far"
        )(held(far), held(first))
    even_part = pl.pallas_call(
        functools.partial(even_kernel, cols),
        out_shape=(vmem(80), vmem(128), vmem(128)),
        scratch_shapes=[pltpu.VMEM((208, 128), F32)],
        compiler_params=pltpu.CompilerParams(vmem_limit_bytes=16 * 1024 * 1024),
        cost_estimate=cost(EVEN_US),
        name="even_set",
    )(*[held(x) for x in (*own, corner, rest, even, mate)])
    out = jax.ShapeDtypeStruct((128, 256), F32)
    grads = pl.pallas_call(
        functools.partial(odd_kernel, cols),
        out_shape=(out, out, out),
        scratch_shapes=[pltpu.VMEM((192, 128), F32), pltpu.VMEM((6, 128, 128), F32)],
        compiler_params=pltpu.CompilerParams(vmem_limit_bytes=16 * 1024 * 1024),
        name="odd_set",
    )(*[held(x) for x in (*own, corner, odd, odd_rest, far, *even_part)])
    return tuple(g.reshape(shape) for g in grads)


def solution(mesh):
    spec = P(None, "ha", "wa", None)
    return jax.shard_map(
        per_device,
        mesh=mesh,
        in_specs=(spec,) * 4,
        out_specs=(spec,) * 3,
        check_vma=False,
    )
```

time: 20.6 us -> 19.1 us (0.927)
  starting transfers between devices: 10.6 us -> 9.76 us
  Pallas kernels: 5.96 us -> 5.18 us
    ppermute x5, waiting for transfers between devices: 1.33 us -> 3.26 us  [the longest x1 1.67 us: per_device(): first = lax.ppermute(to_corner, both, first_pairs)]
    ppermute x1, waiting for transfers between devices: 1.85 us -> 0.01 us  [per_device(): rest = lax.ppermute(to_rest, 'ha', across)]
    pallas_call x1, Pallas kernels: 2.11 us -> 1.52 us  [per_device(): pl.pallas_call(functools.partial(even_kernel, cols), out_shape=(vmem(80),...]
    ppermute x5, starting transfers between devices: 10.1 us -> 9.58 us  [the longest x1 3 us: per_device(): first = lax.ppermute(to_corner, both, first_pairs)]
    ppermute x1, starting transfers between devices: 0.53 us -> 0.09 us  [per_device(): rest = lax.ppermute(to_rest, 'ha', across)]
    pallas_call x1, Pallas kernels: 2.43 us -> 2.06 us  [per_device(): pl.pallas_call(functools.partial(odd_kernel, cols), out_shape=(out, out,...]
    pallas_call x1 -> x6, Pallas kernels: 1.42 us -> 1.6 us  [the longest x1 1.21 us: per_device(): pl.pallas_call(corner_kernel, out_shape=(vmem(184), pltpu.VMEM((8, 128, 1...]
  transfers between devices with their start and end apart: 7 -> 7, of which waited for: 2 -> 2; matrix products, arithmetic and copies ran while one was open for 0% -> 0% of each run, Pallas kernels for 10% -> 2%
where the time goes in v1:
time: 19.1 us; the launch traced here: 18.9 us
  starting transfers between devices  9.76 us (51%)
  Pallas kernels  5.18 us (27%)
  waiting for transfers between devices  3.27 us (17%)
  between operations  0.7 us (4%)
    ppermute x1, starting transfers between devices, per_device(): first = lax.ppermute(to_corner, both, first_pairs)  3 us
    ppermute x1, starting transfers between devices, per_device(): mate = lax.ppermute(to_mate, 'wa', even_pairs)  2.18 us
    pallas_call x1, Pallas kernels, per_device(): pl.pallas_call(functools.partial(odd_kernel, cols), out_shape=(out, out,...  2.06 us
    ppermute x1, starting transfers between devices, per_device(): odd_rest = lax.ppermute(to_odd_rest, both, odd_pairs)  2 us
    ppermute x1, starting transfers between devices, per_device(): far = lax.ppermute(first, both, far_pairs)  1.74 us
    ppermute x1, waiting for transfers between devices, per_device(): first = lax.ppermute(to_corner, both, first_pairs)  1.67 us
    ppermute x1, waiting for transfers between devices, per_device(): far = lax.ppermute(first, both, far_pairs)  1.58 us
    pallas_call x1, Pallas kernels, per_device(): pl.pallas_call(functools.partial(even_kernel, cols), out_shape=(vmem(80),...  1.52 us
  transfers between devices with their start and end apart: 7, of which 2 were waited for; matrix products, arithmetic and copies ran while one was open for 0% of the time, Pallas kernels for 2%

profile of v1, /device:TPU:0, one launch (start us, length us, event | category | flops | bytes accessed | tf_op | source)
XLA Modules:
  0.0 18.9 jit_solution(4295764950270840180)
XLA Ops:
  0.6 1.2 %corner.1 = (f32[184,256]{1,0:T(8,128)S(1)}, f32[8,128,128]{2,1,0:T(8,128)S(1)}) custom-call(f32[128,256]{1,0:T(8,128)} %bitcast.7, f32[128,256]{1,0:T(8,128)} %bitcast.8, f32[128,256]{1,0:T(8,128)} %bitcast.9, f32[128,256]{1,0:T(8,128)} %bitcast.10), custom_call_target="tpu_custom_call" | custom-call | tf_op jit(solution)/shard_map/corner/pallas_call | solution.py:472
  1.8 3.0 %collective-permute-start = (f32[184,256]{1,0:T(8,128)S(1)}, f32[184,256]{1,0:T(8,128)S(1)}, u32[]{:S(2)}, u32[]{:S(2)}) collective-permute-start(f32[184,256]{1,0:T(8,128)S(1)} %get-tuple-element.26), channel_id=1, source_target_pairs={{0,16},{1,17},{2,18},{3,4},{4,3},{5,21},{6,22},{7,8},{8,7},{9,25},... | collective-permute-start | bytes 565256 | tf_op jit(solution)/shard_map/ppermute | solution.py:496
  4.8 0.7 %collective-permute-start.1 = (f32[184,256]{1,0:T(8,128)S(1)}, f32[184,256]{1,0:T(8,128)S(1)}, u32[]{:S(2)}, u32[]{:S(2)}) collective-permute-start(f32[184,256]{1,0:T(8,128)S(1)} %get-tuple-element.26), channel_id=1, source_target_pairs={{0,0},{1,2},{2,1},{3,19},{4,20},{5,6},{6,5},{7,23},{8,24},{9,10},{... | collective-permute-start | bytes 565256 | tf_op jit(solution)/shard_map/ppermute | solution.py:497
  5.5 0.3 %pack.1 = (f32[112,256]{1,0:T(8,128)S(1)}, f32[112,256]{1,0:T(8,128)S(1)}, f32[288,256]{1,0:T(8,128)S(1)}, f32[128,256]{1,0:T(8,128)S(1)}, f32[128,256]{1,0:T(8,...) custom-call(f32[8,128,128]{2,1,0:T(8,128)S(1)} %get-tuple-element.21.split_ref), custom_call_target="tpu_custom_call" | custom-call | tf_op jit(solution)/shard_map/pack/pallas_call | solution.py:475
  5.8 0.1 collective-permute-start.2
  5.9 2.0 %collective-permute-start.3 = (f32[112,256]{1,0:T(8,128)S(1)}, f32[112,256]{1,0:T(8,128)S(1)}, u32[]{:S(2)}, u32[]{:S(2)}) collective-permute-start(f32[112,256]{1,0:T(8,128)S(1)} %get-tuple-element.30), channel_id=1, source_target_pairs={{0,16},{1,2},{2,1},{3,4},{4,3},{5,6},{6,5},{7,8},{8,7},{9,10},{10,... | collective-permute-start | bytes 344072 | tf_op jit(solution)/shard_map/ppermute | solution.py:499
  7.9 1.7 %collective-permute-done.first_ref.gate_ref = f32[184,256]{1,0:T(8,128)S(1)} collective-permute-done((f32[184,256]{1,0:T(8,128)S(1)}, f32[184,256]{1,0:T(8,128)S(1)}, u32[]{:S(2)}, u32[]{:S(2)}) %collective-permute-start) | collective-permute-done | bytes 188448 | tf_op jit(solution)/shard_map/ppermute | solution.py:496
  9.6 1.7 %collective-permute-start.4 = (f32[184,256]{1,0:T(8,128)S(1)}, f32[184,256]{1,0:T(8,128)S(1)}, u32[]{:S(2)}, u32[]{:S(2)}) collective-permute-start(f32[184,256]{1,0:T(8,128)S(1)} %collective-permute-done.first_ref.gate_ref), channel_id=1, source_target_pairs={{0,16},{1,2},{2,1},{3,19},{4,20},{5,6},{6,5},{7,23},{8,24},{9,10},... | collective-permute-start | bytes 565256 | tf_op jit(solution)/shard_map/ppermute | solution.py:502
  11.3 0.0 collective-permute-done.2.rest_ref
  11.3 0.0 collective-permute-done.1.second_ref
  11.3 0.1 sort.1
  11.4 2.2 %collective-permute-start.6 = (f32[296,256]{1,0:T(8,128)S(1)}, f32[296,256]{1,0:T(8,128)S(1)}, u32[]{:S(2)}, u32[]{:S(2)}) collective-permute-start(f32[296,256]{1,0:T(8,128)S(1)} %get-tuple-element.32), channel_id=1, source_target_pairs={{0,1},{1,0},{2,3},{3,2},{4,5},{5,4},{6,7},{7,6},{8,9},{9,8},{10,11... | collective-permute-start | bytes 909320 | tf_op jit(solution)/shard_map/ppermute | solution.py:506
  13.6 0.1 collective-permute-start.5
  13.7 0.0 collective-permute-done.3.message_ref
  13.7 1.6 %collective-permute-done.4.message_ref = f32[184,256]{1,0:T(8,128)S(1)} collective-permute-done((f32[184,256]{1,0:T(8,128)S(1)}, f32[184,256]{1,0:T(8,128)S(1)}, u32[]{:S(2)}, u32[]{:S(2)}) %collective-permute-start.4) | collective-permute-done | bytes 188448 | tf_op jit(solution)/shard_map/ppermute | solution.py:502
  15.3 0.0 collective-permute-done.5.even_ref
  15.3 0.0 collective-permute-done.6.mate_ref
  15.3 1.5 %even_set.1 = (f32[80,256]{1,0:T(8,128)S(1)}, f32[128,256]{1,0:T(8,128)S(1)}, f32[128,256]{1,0:T(8,128)S(1)}) custom-call(f32[128,256]{1,0:T(8,128)S(1)} %get-tuple-element.22.own_q_ref, f32[128,256]{1,0:T(8,128)S(1)} %get-tuple-element.23.own_k_ref, f32[128,256]{1,0:T(8,128)S(1)} %get-tuple-element.24.own_v_ref, ...), custom_call_target="tpu_custom_call" | custom-call | tf_op jit(solution)/shard_map/even_set/pallas_call | solution.py:516
  16.8 2.1 %odd_set.1 = (f32[128,256]{1,0:T(8,128)}, f32[128,256]{1,0:T(8,128)}, f32[128,256]{1,0:T(8,128)}) custom-call(f32[128,256]{1,0:T(8,128)S(1)} %get-tuple-element.22.own_q_ref, f32[128,256]{1,0:T(8,128)S(1)} %get-tuple-element.23.own_k_ref, f32[128,256]{1,0:T(8,128)S(1)} %get-tuple-element.24.own_v_ref, f32[128,256]{1,0:T(8,128)S(1)} %get-tuple-element.25.own_c_ref, ...), custom_call_target="tpu_custom_call" | custom-call | tf_op jit(solution)/shard_map/odd_set/pallas_call | solution.py:525
  (3 shorter events, 0.0 us)
Async XLA Ops:
  1.8 7.7 %collective-permute-start = (f32[184,256]{1,0:T(8,128)S(1)}, f32[184,256]{1,0:T(8,128)S(1)}, u32[]{:S(2)}, u32[]{:S(2)}) collective-permute-start(f32[184,256]{1,0:T(8,128)S(1)} %get-tuple-element.26), channel_id=1, source_target_pairs={{0,16},{1,17},{2,18},{3,4},{4,3},{5,21},{6,22},{7,8},{8,7},{9,25},... | collective-permute-start | bytes 565256 | tf_op jit(solution)/shard_map/ppermute | solution.py:496
  4.8 6.5 %collective-permute-start.1 = (f32[184,256]{1,0:T(8,128)S(1)}, f32[184,256]{1,0:T(8,128)S(1)}, u32[]{:S(2)}, u32[]{:S(2)}) collective-permute-start(f32[184,256]{1,0:T(8,128)S(1)} %get-tuple-element.26), channel_id=1, source_target_pairs={{0,0},{1,2},{2,1},{3,19},{4,20},{5,6},{6,5},{7,23},{8,24},{9,10},{... | collective-permute-start | bytes 565256 | tf_op jit(solution)/shard_map/ppermute | solution.py:497
  5.8 5.5 %collective-permute-start.2 = (f32[112,256]{1,0:T(8,128)S(1)}, f32[112,256]{1,0:T(8,128)S(1)}, u32[]{:S(2)}, u32[]{:S(2)}) collective-permute-start(f32[112,256]{1,0:T(8,128)S(1)} %get-tuple-element.27), channel_id=1, source_target_pairs={{0,16},{16,0},{1,17},{17,1},{2,18},{18,2},{3,19},{19,3},{4,20},{20... | collective-permute-start | bytes 344072 | tf_op jit(solution)/shard_map/ppermute | solution.py:498
  5.9 7.8 %collective-permute-start.3 = (f32[112,256]{1,0:T(8,128)S(1)}, f32[112,256]{1,0:T(8,128)S(1)}, u32[]{:S(2)}, u32[]{:S(2)}) collective-permute-start(f32[112,256]{1,0:T(8,128)S(1)} %get-tuple-element.30), channel_id=1, source_target_pairs={{0,16},{1,2},{2,1},{3,4},{4,3},{5,6},{6,5},{7,8},{8,7},{9,10},{10,... | collective-permute-start | bytes 344072 | tf_op jit(solution)/shard_map/ppermute | solution.py:499
  9.6 5.7 %collective-permute-start.4 = (f32[184,256]{1,0:T(8,128)S(1)}, f32[184,256]{1,0:T(8,128)S(1)}, u32[]{:S(2)}, u32[]{:S(2)}) collective-permute-start(f32[184,256]{1,0:T(8,128)S(1)} %collective-permute-done.first_ref.gate_ref), channel_id=1, source_target_pairs={{0,16},{1,2},{2,1},{3,19},{4,20},{5,6},{6,5},{7,23},{8,24},{9,10},... | collective-permute-start | bytes 565256 | tf_op jit(solution)/shard_map/ppermute | solution.py:502
  11.4 3.9 %collective-permute-start.6 = (f32[296,256]{1,0:T(8,128)S(1)}, f32[296,256]{1,0:T(8,128)S(1)}, u32[]{:S(2)}, u32[]{:S(2)}) collective-permute-start(f32[296,256]{1,0:T(8,128)S(1)} %get-tuple-element.32), channel_id=1, source_target_pairs={{0,1},{1,0},{2,3},{3,2},{4,5},{5,4},{6,7},{7,6},{8,9},{9,8},{10,11... | collective-permute-start | bytes 909320 | tf_op jit(solution)/shard_map/ppermute | solution.py:506
  13.6 1.7 %collective-permute-start.5 = (f32[288,256]{1,0:T(8,128)S(1)}, f32[288,256]{1,0:T(8,128)S(1)}, u32[]{:S(2)}, u32[]{:S(2)}) collective-permute-start(f32[288,256]{1,0:T(8,128)S(1)} %release.1), channel_id=1, source_target_pairs={{0,1},{1,0},{2,3},{3,2},{4,5},{5,4},{6,7},{7,6},{8,9},{9,8},{10,11... | collective-permute-start | bytes 884744 | tf_op jit(solution)/shard_map/ppermute | solution.py:501

commit v2 on v1

--- a/solution.py
+++ b/solution.py
@@ -187,6 +187,9 @@
     token_c = jnp.full((8, 128), 3 * FAR, jnp.int32)
     first = 0
     for place, real, count in token_segments:
+        if place is None:
+            first += count
+            continue
         r, c = place(jnp.clip(lane - first, 0, real - 1))
         inside = jnp.logical_and(lane >= first, lane < first + real)
         token_r = jnp.where(inside, r, token_r)
@@ -252,10 +255,7 @@
                         side(low, hi, hi, upper).astype(BF),
                         side(low, lo, lo, upper).astype(BF),
                     ]
-            whole = jnp.concatenate(pieces, axis=1)
-            if not left:
-                whole = jnp.concatenate([whole, jnp.zeros((128 - whole.shape[0], whole.shape[1]), BF)], axis=0)
-            out.append(whole)
+            out.append(jnp.concatenate(pieces, axis=1))
     return out
 
 
@@ -333,57 +333,137 @@
 SIDE = (0, 48, 96, 120)
 
 
-def even_kernel(cols, own_q_ref, own_k_ref, own_v_ref, own_c_ref, corner_ref, rest_ref, even_ref, mate_ref, dq_ref, dk_ref, dv_ref, bias_ref):
+def keep(ref, image, parts):
+    count = parts[0].shape[0]
+    for head in range(HEADS):
+        first = (HEADS * image + head) * count
+        ref[first : first + count, :] = parts[head]
+
+
+def joined(image, refs, late, rows):
+    out = []
+    for head in range(HEADS):
+        parts = []
+        for ref, take in refs:
+            count = ref.shape[0] // (2 * HEADS)
+            first = (HEADS * image + head) * count
+            parts.append(ref[first : first + take, :])
+        parts.append(late[head])
+        have = sum(x.shape[0] for x in parts)
+        if have < rows:
+            parts.append(jnp.zeros((rows - have, late[head].shape[1]), BF))
+        out.append(jnp.concatenate(parts, axis=0))
+    return out
+
+
+def own_kernel(cols, own_q_ref, own_k_ref, own_v_ref, own_c_ref, even_bias_ref, odd_bias_ref, k_ref, v_ref, q_ref, c_ref):
     at = Places(cols)
     write_bias(
-        bias_ref,
-        ((at.own, 64, 64), (at.ha_in, 24, 24), (at.even_inner, 24, 24), (at.deven_in, 24, 24),
-         (at.ha_out, 24, 24), (at.even_outer, 24, 24), (at.deven_out, 24, 24)),
-        ((lambda i: at.own(i, 3), 40, 40), (lambda i: at.ha_in(i, 3), 15, 16), (at.even_inner, 24, 24),
+        even_bias_ref,
+        ((at.own, 64, 64), (at.ha_in, 24, 24), (at.ha_out, 24, 24), (at.even_inner, 24, 24), (at.even_outer, 24, 24),
+         (at.deven_in, 24, 24), (at.deven_out, 24, 24)),
+        ((None, 0, 24), (lambda i: at.own(i, 3), 40, 40), (lambda i: at.ha_in(i, 3), 15, 16), (at.even_inner, 24, 24),
          (at.deven_in, 24, 24)),
     )
+    write_bias(
+        odd_bias_ref,
+        ((at.own, 48, 48), (at.ha_in, 18, 24), (at.ha_out, 18, 24), (at.odd_inner, 24, 24), (at.odd_outer, 24, 24),
+         (at.dodd_in, 9, 16), (at.dodd_out, 27, 32)),
+        ((at.own, 24, 32), (at.ha_in, 9, 16), (at.odd_tokens, 24, 32), (at.dodd_in, 9, 16)),
+    )
+    for image in range(2):
+        here = slice(64 * image, 64 * image + 64)
+        keep(k_ref, image, stacked(own_k_ref[here, :], True, 3))
+        keep(v_ref, image, stacked(own_v_ref[here, :], True, 2))
+        keep(q_ref, image, stacked(own_q_ref[here, :] * 0.125, False, 3))
+        keep(c_ref, image, stacked(own_c_ref[here, :], False, 2))
+
+
+def ha_inner(image, corner_ref, rest_ref, field):
+    return rows(corner_ref, 90 * image + CORNER[field], 18) + rows(rest_ref, 54 * image + REST[field], 6)
+
+
+def ha_outer(image, corner_ref, rest_ref, field):
+    return rows(corner_ref, 90 * image + CORNER[field] + 18, 18) + rows(rest_ref, 54 * image + REST[field] + 6, 6)
+
+
+def odd_inner(image, odd_ref, odd_rest_ref, field):
+    corner, rest = 90 * image + CORNER[field], 54 * image + REST[field]
+    return rows(odd_ref, corner, 9) + rows(odd_ref, corner + 18, 9) + rows(odd_rest_ref, rest, 6)
+
+
+def odd_outer(image, odd_ref, odd_rest_ref, field):
+    corner, rest = 90 * image + CORNER[field], 54 * image + REST[field]
+    return rows(odd_ref, corner + 9, 9) + rows(odd_ref, corner + 27, 9) + rows(odd_rest_ref, rest + 6, 6)
+
+
+def odd_middle_tokens(image, corner_ref, odd_ref, odd_rest_ref, field):
+    corner, rest = 90 * image + CORNER[field], 54 * image + REST[field]
+    return rows(corner_ref, corner, 9, 7) + rows(odd_ref, corner, 9) + rows(odd_rest_ref, rest, 15, 8)
+
+
+def middle_kernel(corner_ref, rest_ref, odd_ref, odd_rest_ref, even_k_ref, even_v_ref, even_q_ref, even_c_ref,
+                  odd_k_ref, odd_v_ref, odd_q_ref, odd_c_ref):
+    for image in range(2):
+        for field, even_ref, odd_to_ref, parts in ((0, even_k_ref, odd_k_ref, 3), (1, even_v_ref, odd_v_ref, 2)):
+            corner = 90 * image + CORNER[field]
+            x = ha_inner(image, corner_ref, rest_ref, field) + ha_outer(image, corner_ref, rest_ref, field)
+            keep(even_ref, image, stacked(jnp.concatenate(x, axis=0), True, parts))
+            x = rows(corner_ref, corner, 18, 6) + rows(corner_ref, corner + 18, 18, 6)
+            x += odd_inner(image, odd_ref, odd_rest_ref, field) + odd_outer(image, odd_ref, odd_rest_ref, field)
+            keep(odd_to_ref, image, stacked(jnp.concatenate(x, axis=0), True, parts))
+        for field, even_ref, odd_to_ref, parts, scale in (
+            (2, even_q_ref, odd_q_ref, 3, 0.125), (3, even_c_ref, odd_c_ref, 2, 1.0),
+        ):
+            x = jnp.concatenate(rows(rest_ref, 54 * image + REST[field], 15, 1), axis=0)
+            keep(even_ref, image, stacked(x * scale, False, parts))
+            x = jnp.concatenate(odd_middle_tokens(image, corner_ref, odd_ref, odd_rest_ref, field), axis=0)
+            keep(odd_to_ref, image, stacked(x * scale, False, parts))
+
+
+def even_kernel(own_q_ref, own_k_ref, own_c_ref, corner_ref, rest_ref, even_ref, mate_ref, bias_ref,
+                k0_ref, v0_ref, q0_ref, c0_ref, k1_ref, v1_ref, q1_ref, c1_ref, dq_ref, dk_ref, dv_ref):
     work = []
     for image in range(2):
 
-        def keys(own_ref, field):
-            corner, rest, even = 90 * image + CORNER[field], 54 * image + REST[field], 144 * image + SIDE[field]
-            out = rows(own_ref, 64 * image, 64)
-            out += rows(corner_ref, corner, 18) + rows(rest_ref, rest, 6)
-            out += rows(even_ref, even, 24)
-            out += rows(mate_ref, corner, 18) + rows(mate_ref, 184 + rest, 6)
-            out += rows(corner_ref, corner + 18, 18) + rows(rest_ref, rest + 6, 6)
-            out += rows(even_ref, even + 24, 24)
-            out += rows(mate_ref, corner + 18, 18) + rows(mate_ref, 184 + rest + 6, 6)
+        def mate_inner(field):
+            return rows(mate_ref, 90 * image + CORNER[field], 18) + rows(mate_ref, 184 + 54 * image + REST[field], 6)
+
+        def late_keys(field):
+            even = 144 * image + SIDE[field]
+            out = rows(even_ref, even, 48) + mate_inner(field)
+            out += rows(mate_ref, 90 * image + CORNER[field] + 18, 18)
+            out += rows(mate_ref, 184 + 54 * image + REST[field] + 6, 6)
             return jnp.concatenate(out, axis=0)
 
-        def tokens(own_ref, field):
-            corner, rest, even = 90 * image + CORNER[field], 54 * image + REST[field], 144 * image + SIDE[field]
-            out = rows(own_ref, 64 * image + 24, 40)
-            out += rows(rest_ref, rest, 15, 1)
-            out += rows(even_ref, even, 24)
-            out += rows(mate_ref, corner, 9) + rows(mate_ref, 184 + rest, 15, 8)
+        def late_tokens(field):
+            out = rows(even_ref, 144 * image + SIDE[field], 24)
+            out += rows(mate_ref, 90 * image + CORNER[field], 9) + rows(mate_ref, 184 + 54 * image + REST[field], 15)
             return jnp.concatenate(out, axis=0)
 
-        key, query, cot = keys(own_k_ref, 0), tokens(own_q_ref, 2) * 0.125, tokens(own_c_ref, 3)
+        late_q, late_c = late_tokens(2) * 0.125, late_tokens(3)
+        key = rows(own_k_ref, 64 * image, 64) + ha_inner(image, corner_ref, rest_ref, 0)
+        key += rows(even_ref, 144 * image, 24) + mate_inner(0)
+        query = rows(own_q_ref, 64 * image, 64) + rows(rest_ref, 54 * image + REST[2], 15, 1)
+        cot = rows(own_c_ref, 64 * image, 64) + rows(rest_ref, 54 * image + REST[3], 15, 1)
         work.append((
-            stacked(key, True, 3), stacked(keys(own_v_ref, 1), True, 2), stacked(query, False, 3), stacked(cot, False, 2),
-            key[0:136], query, cot,
+            joined(image, ((k0_ref, 64), (k1_ref, 48)), stacked(late_keys(0), True, 3), 208),
+            joined(image, ((v0_ref, 64), (v1_ref, 48)), stacked(late_keys(1), True, 2), 208),
+            joined(image, ((q0_ref, 64), (q1_ref, 16)), stacked(late_q, False, 3), 128),
+            joined(image, ((c0_ref, 64), (c1_ref, 16)), stacked(late_c, False, 2), 128),
+            jnp.concatenate(key, axis=0),
+            jnp.concatenate([jnp.concatenate(query, axis=0) * 0.125, late_q], axis=0),
+            jnp.concatenate(cot + [late_c], axis=0),
         ))
-    for image, (dq, dk, dv) in enumerate(attend(work, bias_ref, 40, 64, (slice(0, 136),))):
-        dq_ref[40 * image : 40 * image + 40, :] = dq
-        dk_ref[64 * image : 64 * image + 64, :] = dk
-        dv_ref[64 * image : 64 * image + 64, :] = dv
-
-
-def early_tokens(image, own_ref, corner_ref, odd_ref, odd_rest_ref, field):
-    corner, rest = 90 * image + CORNER[field], 54 * image + REST[field]
-    out = rows(own_ref, 64 * image, 24)
-    out += rows(corner_ref, corner, 9, 7)
-    out += rows(odd_ref, corner, 9) + rows(odd_rest_ref, rest, 15)
-    return jnp.concatenate(out, axis=0)
-
-
-def sort_kernel(cols, first_ref, second_ref, rest_ref, ha_ref, odd_ref, mate_ref):
+    parts = attend(work, bias_ref, 64, 64, (slice(0, 88), slice(112, 136), slice(160, 184)))
+    for image, (dq, dk, dv) in enumerate(parts):
+        here = slice(64 * image, 64 * image + 64)
+        dq_ref[here, :] = dq
+        dk_ref[here, :] = dk
+        dv_ref[here, :] = dv
+
+
+def sort_kernel(cols, first_ref, second_ref, rest_ref, gate_ref, ha_ref, odd_ref, mate_ref):
     turned = by_row(lax.axis_index("wa"), cols)
     first, second = first_ref[...], second_ref[...]
     ha = jnp.where(turned, second, first)
@@ -401,48 +481,41 @@
     return jnp.logical_and(((w + 1) >> 1) % 2 == 0, jnp.logical_and(w > 0, w < cols - 1))
 
 
-def odd_kernel(cols, own_q_ref, own_k_ref, own_v_ref, own_c_ref, corner_ref, odd_ref, odd_rest_ref, far_ref, even_dq_ref,
-               even_dk_ref, even_dv_ref, dq_ref, dk_ref, dv_ref, bias_ref, split_ref):
-    at = Places(cols)
-    p = at.p
-    write_bias(
-        bias_ref,
-        ((at.own, 48, 48), (at.ha_in, 18, 24), (at.odd_inner, 24, 24), (at.ha_out, 18, 24), (at.odd_outer, 24, 24),
-         (at.dodd_in, 9, 16), (at.dodd_out, 27, 32)),
-        ((at.own, 24, 24), (at.ha_in, 9, 16), (at.odd_tokens, 24, 24), (at.dodd_in, 9, 16)),
-    )
+def odd_kernel(own_q_ref, own_k_ref, own_c_ref, corner_ref, odd_ref, odd_rest_ref, far_ref, even_dq_ref, even_dk_ref,
+               even_dv_ref, bias_ref, k0_ref, v0_ref, q0_ref, c0_ref, k1_ref, v1_ref, q1_ref, c1_ref,
+               dq_ref, dk_ref, dv_ref, split_ref):
+    p = lax.axis_index("wa") % 2
     work = []
     for image in range(2):
 
-        def keys(own_ref, field):
-            corner, rest = 90 * image + CORNER[field], 54 * image + REST[field]
-            out = rows(own_ref, 64 * image, 48)
-            out += rows(corner_ref, corner, 18, 6)
-            out += rows(odd_ref, corner, 9) + rows(odd_ref, corner + 18, 9) + rows(odd_rest_ref, rest, 6)
-            out += rows(corner_ref, corner + 18, 18, 6)
-            out += rows(odd_ref, corner + 9, 9) + rows(odd_ref, corner + 27, 9) + rows(odd_rest_ref, rest + 6, 6)
-            out += rows(far_ref, corner, 9, 7) + rows(far_ref, corner + 9, 27, 5)
-            return jnp.concatenate(out, axis=0)
-
-        def tokens(own_ref, field):
-            corner, rest = 90 * image + CORNER[field], 54 * image + REST[field]
-            out = rows(own_ref, 64 * image, 24)
-            out += rows(corner_ref, corner, 9, 7)
-            out += rows(odd_ref, corner, 9) + rows(odd_rest_ref, rest, 15)
-            out += rows(far_ref, corner, 9, 7)
-            return jnp.concatenate(out, axis=0)
-
-        key, query, cot = keys(own_k_ref, 0), tokens(own_q_ref, 2) * 0.125, tokens(own_c_ref, 3)
+        def late_keys(field):
+            corner = 90 * image + CORNER[field]
+            return jnp.concatenate(rows(far_ref, corner, 9, 7) + rows(far_ref, corner + 9, 27, 5), axis=0)
+
+        def late_tokens(field):
+            return jnp.concatenate(rows(far_ref, 90 * image + CORNER[field], 9, 7), axis=0)
+
+        late_q, late_c = late_tokens(2) * 0.125, late_tokens(3)
+        late_k = late_keys(0)
+        key = rows(own_k_ref, 64 * image, 48) + rows(corner_ref, 90 * image, 18, 6)
+        key += odd_inner(image, odd_ref, odd_rest_ref, 0) + [late_k[0:16]]
+        query = rows(own_q_ref, 64 * image, 32) + odd_middle_tokens(image, corner_ref, odd_ref, odd_rest_ref, 2)
+        cot = rows(own_c_ref, 64 * image, 32) + odd_middle_tokens(image, corner_ref, odd_ref, odd_rest_ref, 3)
         work.append((
-            stacked(key, True, 3), stacked(keys(own_v_ref, 1), True, 2), stacked(query, False, 3), stacked(cot, False, 2),
-            jnp.concatenate([key[0:96], key[144:160]], axis=0), query, cot,
+            joined(image, ((k0_ref, 48), (k1_ref, 96)), stacked(late_k, True, 3), 192),
+            joined(image, ((v0_ref, 48), (v1_ref, 96)), stacked(late_keys(1), True, 2), 192),
+            joined(image, ((q0_ref, 32), (q1_ref, 48)), stacked(late_q, False, 3), 128),
+            joined(image, ((c0_ref, 32), (c1_ref, 48)), stacked(late_c, False, 2), 128),
+            jnp.concatenate(key, axis=0),
+            jnp.concatenate([jnp.concatenate(query, axis=0) * 0.125, late_q], axis=0),
+            jnp.concatenate(cot + [late_c], axis=0),
         ))
-    parts = attend(work, bias_ref, 24, 48, (slice(0, 96), slice(144, 160)))
+    parts = attend(work, bias_ref, 24, 48, (slice(0, 72), slice(96, 120), slice(144, 160)))
     for image, (dq, dk, dv) in enumerate(parts):
         here = slice(64 * image, 64 * image + 64)
         none = jnp.zeros((16, 256), F32)
         results = (
-            jnp.concatenate([dq, even_dq_ref[40 * image : 40 * image + 40, :]], axis=0),
+            jnp.concatenate([dq, jnp.zeros((40, 256), F32)], axis=0) + even_dq_ref[here, :],
             jnp.concatenate([dk, none], axis=0) + even_dk_ref[here, :],
             jnp.concatenate([dv, none], axis=0) + even_dv_ref[here, :],
         )
@@ -456,6 +529,8 @@
             ref[:, 128 * half : 128 * half + 128] = split_ref[2 * index + half]
 
 
+SMALL = pltpu.CompilerParams(vmem_limit_bytes=6 * 1024 * 1024)
+OWN_US = 1
 PREP_US = 1
 FAR_US = 2
 EVEN_US = 0
@@ -470,10 +545,10 @@
     cols = lax.axis_size("wa")
     flat = [x.reshape(128, 256) for x in (queries, keys, values, cotangent)]
     to_corner, split = pl.pallas_call(
-        corner_kernel, out_shape=(vmem(184), pltpu.VMEM((8, 128, 128), F32)), name="corner"
+        corner_kernel, out_shape=(vmem(184), pltpu.VMEM((8, 128, 128), F32)), name="corner",
     )(flat[1], flat[2], flat[0], flat[3])
     to_rest, to_odd_rest, to_even, own_k, own_v, own_q, own_c = pl.pallas_call(
-        pack_kernel, out_shape=(vmem(112), vmem(112), vmem(288)) + (vmem(128),) * 4, name="pack"
+        pack_kernel, out_shape=(vmem(112), vmem(112), vmem(288)) + (vmem(128),) * 4, name="pack", compiler_params=SMALL,
     )(held(split))
     own = (own_q, own_k, own_v, own_c)
 
@@ -497,38 +572,52 @@
     second = lax.ppermute(to_corner, both, second_pairs)
     rest = lax.ppermute(to_rest, "ha", across)
     odd_rest = lax.ppermute(to_odd_rest, both, odd_pairs)
-    to_even = pl.pallas_call(release_kernel, out_shape=vmem(288), name="release")(held(to_even), held(first))
+    to_even = pl.pallas_call(release_kernel, out_shape=vmem(288), name="release", compiler_params=SMALL)(held(to_even), held(first))
     even = lax.ppermute(to_even, "wa", even_pairs)
     far = lax.ppermute(first, both, far_pairs)
+    each = 2 * HEADS
+
+    def stacks(key_rows, token_rows):
+        return (vmem(each * key_rows, 384, BF), vmem(each * key_rows, 256, BF), vmem(each * token_rows, 384, BF),
+                vmem(each * token_rows, 256, BF))
+
+    even_bias, odd_bias, *own_stacks = pl.pallas_call(
+        functools.partial(own_kernel, cols),
+        out_shape=(vmem(208, 128), vmem(192, 128)) + stacks(64, 64),
+        compiler_params=SMALL,
+        cost_estimate=cost(OWN_US),
+        name="own",
+    )(*[held(x) for x in own])
     corner, odd, to_mate = pl.pallas_call(
-        functools.partial(sort_kernel, cols), out_shape=(vmem(184), vmem(184), vmem(296)), name="sort"
-    )(*[held(x) for x in (first, second, rest)])
+        functools.partial(sort_kernel, cols), out_shape=(vmem(184), vmem(184), vmem(296)), name="sort", compiler_params=SMALL,
+    )(*[held(x) for x in (first, second, rest, even_bias)])
     mate = lax.ppermute(to_mate, "wa", even_pairs)
-
-    if PREP_US:
-        odd_rest = pl.pallas_call(
-            release_kernel, out_shape=vmem(112), cost_estimate=cost(PREP_US), name="arrive"
-        )(held(odd_rest), held(first))
+    middle = pl.pallas_call(
+        middle_kernel,
+        out_shape=stacks(48, 16) + stacks(96, 48),
+        compiler_params=SMALL,
+        cost_estimate=cost(PREP_US),
+        name="middle",
+    )(*[held(x) for x in (corner, rest, odd, odd_rest)])
     if FAR_US:
         far = pl.pallas_call(
-            release_kernel, out_shape=vmem(184), cost_estimate=cost(FAR_US), name="arrive_far"
+            release_kernel, out_shape=vmem(184), cost_estimate=cost(FAR_US), name="arrive_far", compiler_params=SMALL,
         )(held(far), held(first))
     even_part = pl.pallas_call(
-        functools.partial(even_kernel, cols),
-        out_shape=(vmem(80), vmem(128), vmem(128)),
-        scratch_shapes=[pltpu.VMEM((208, 128), F32)],
-        compiler_params=pltpu.CompilerParams(vmem_limit_bytes=16 * 1024 * 1024),
+        even_kernel,
+        out_shape=(vmem(128), vmem(128), vmem(128)),
+        compiler_params=SMALL,
         cost_estimate=cost(EVEN_US),
         name="even_set",
-    )(*[held(x) for x in (*own, corner, rest, even, mate)])
+    )(*[held(x) for x in (own_q, own_k, own_c, corner, rest, even, mate, even_bias, *own_stacks, *middle[0:4])])
     out = jax.ShapeDtypeStruct((128, 256), F32)
     grads = pl.pallas_call(
-        functools.partial(odd_kernel, cols),
+        odd_kernel,
         out_shape=(out, out, out),
-        scratch_shapes=[pltpu.VMEM((192, 128), F32), pltpu.VMEM((6, 128, 128), F32)],
-        compiler_params=pltpu.CompilerParams(vmem_limit_bytes=16 * 1024 * 1024),
+        scratch_shapes=[pltpu.VMEM((6, 128, 128), F32)],
+        compiler_params=SMALL,
         name="odd_set",
-    )(*[held(x) for x in (*own, corner, odd, odd_rest, far, *even_part)])
+    )(*[held(x) for x in (own_q, own_k, own_c, corner, odd, odd_rest, far, *even_part, odd_bias, *own_stacks, *middle[4:8])])
     return tuple(g.reshape(shape) for g in grads)
 
 

time: 19.1 us -> 18.6 us (0.974)
  waiting for transfers between devices: 3.27 us -> 2.86 us
  starting transfers between devices: 9.76 us -> 9.37 us
  Pallas kernels: 5.18 us -> 5.55 us
    ppermute x1, waiting for transfers between devices: 1.58 us -> 1.17 us  [per_device(): far = lax.ppermute(first, both, far_pairs)]
    ppermute x1, starting transfers between devices: 2.18 us -> 1.79 us  [per_device(): mate = lax.ppermute(to_mate, 'wa', even_pairs)]
    pallas_call x4 -> x5, Pallas kernels: 3.61 us -> 3.98 us  [the longest x1 1.8 us: per_device(): pl.pallas_call(odd_kernel, out_shape=(out, out, out), scratch_shapes=[plt...]
  transfers between devices with their start and end apart: 7 -> 7, of which waited for: 2 -> 2; matrix products, arithmetic and copies ran while one was open for 0% -> 0% of each run, Pallas kernels for 2% -> 6%
where the time goes in v2:
time: 18.6 us; the launch traced here: 18.5 us
  starting transfers between devices  9.37 us (50%)
  Pallas kernels  5.55 us (30%)
  waiting for transfers between devices  2.86 us (15%)
  between operations  0.71 us (4%)
    ppermute x1, starting transfers between devices, per_device(): first = lax.ppermute(to_corner, both, first_pairs)  3 us
    ppermute x1, starting transfers between devices, per_device(): odd_rest = lax.ppermute(to_odd_rest, both, odd_pairs)  2 us
    pallas_call x1, Pallas kernels, per_device(): pl.pallas_call(odd_kernel, out_shape=(out, out, out), scratch_shapes=[plt...  1.8 us
    ppermute x1, starting transfers between devices, per_device(): mate = lax.ppermute(to_mate, 'wa', even_pairs)  1.79 us
    ppermute x1, starting transfers between devices, per_device(): far = lax.ppermute(first, both, far_pairs)  1.74 us
    ppermute x1, waiting for transfers between devices, per_device(): first = lax.ppermute(to_corner, both, first_pairs)  1.67 us
    pallas_call x1, Pallas kernels, per_device(): pl.pallas_call(even_kernel, out_shape=(vmem(128), vmem(128), vmem(128)),...  1.37 us
    pallas_call x1, Pallas kernels, per_device(): pl.pallas_call(corner_kernel, out_shape=(vmem(184), pltpu.VMEM((8, 128, 1...  1.21 us
  transfers between devices with their start and end apart: 7, of which 2 were waited for; matrix products, arithmetic and copies ran while one was open for 0% of the time, Pallas kernels for 6%

profile of v2, /device:TPU:0, one launch (start us, length us, event | category | flops | bytes accessed | tf_op | source)
XLA Modules:
  0.0 18.5 jit_solution(2233535099931996028)
XLA Ops:
  0.6 1.2 %corner.1 = (f32[184,256]{1,0:T(8,128)S(1)}, f32[8,128,128]{2,1,0:T(8,128)S(1)}) custom-call(f32[128,256]{1,0:T(8,128)} %bitcast.7, f32[128,256]{1,0:T(8,128)} %bitcast.8, f32[128,256]{1,0:T(8,128)} %bitcast.9, f32[128,256]{1,0:T(8,128)} %bitcast.10), custom_call_target="tpu_custom_call" | custom-call | tf_op jit(solution)/shard_map/corner/pallas_call | solution.py:547
  1.8 3.0 %collective-permute-start = (f32[184,256]{1,0:T(8,128)S(1)}, f32[184,256]{1,0:T(8,128)S(1)}, u32[]{:S(2)}, u32[]{:S(2)}) collective-permute-start(f32[184,256]{1,0:T(8,128)S(1)} %get-tuple-element.39), channel_id=1, source_target_pairs={{0,16},{1,17},{2,18},{3,4},{4,3},{5,21},{6,22},{7,8},{8,7},{9,25},... | collective-permute-start | bytes 565256 | tf_op jit(solution)/shard_map/ppermute | solution.py:571
  4.8 0.7 %collective-permute-start.1 = (f32[184,256]{1,0:T(8,128)S(1)}, f32[184,256]{1,0:T(8,128)S(1)}, u32[]{:S(2)}, u32[]{:S(2)}) collective-permute-start(f32[184,256]{1,0:T(8,128)S(1)} %get-tuple-element.39), channel_id=1, source_target_pairs={{0,0},{1,2},{2,1},{3,19},{4,20},{5,6},{6,5},{7,23},{8,24},{9,10},{... | collective-permute-start | bytes 565256 | tf_op jit(solution)/shard_map/ppermute | solution.py:572
  5.5 0.3 %pack.1 = (f32[112,256]{1,0:T(8,128)S(1)}, f32[112,256]{1,0:T(8,128)S(1)}, f32[288,256]{1,0:T(8,128)S(1)}, f32[128,256]{1,0:T(8,128)S(1)}, f32[128,256]{1,0:T(8,...) custom-call(f32[8,128,128]{2,1,0:T(8,128)S(1)} %get-tuple-element.35.split_ref), custom_call_target="tpu_custom_call" | custom-call | tf_op jit(solution)/shard_map/pack/pallas_call | solution.py:550
  5.8 0.1 collective-permute-start.2
  5.9 2.0 %collective-permute-start.3 = (f32[112,256]{1,0:T(8,128)S(1)}, f32[112,256]{1,0:T(8,128)S(1)}, u32[]{:S(2)}, u32[]{:S(2)}) collective-permute-start(f32[112,256]{1,0:T(8,128)S(1)} %get-tuple-element.45), channel_id=1, source_target_pairs={{0,16},{1,2},{2,1},{3,4},{4,3},{5,6},{6,5},{7,8},{8,7},{9,10},{10,... | collective-permute-start | bytes 344072 | tf_op jit(solution)/shard_map/ppermute | solution.py:574
  7.9 1.7 %collective-permute-done.first_ref.gate_ref = f32[184,256]{1,0:T(8,128)S(1)} collective-permute-done((f32[184,256]{1,0:T(8,128)S(1)}, f32[184,256]{1,0:T(8,128)S(1)}, u32[]{:S(2)}, u32[]{:S(2)}) %collective-permute-start) | collective-permute-done | bytes 188448 | tf_op jit(solution)/shard_map/ppermute | solution.py:571
  9.6 1.7 %collective-permute-start.4 = (f32[184,256]{1,0:T(8,128)S(1)}, f32[184,256]{1,0:T(8,128)S(1)}, u32[]{:S(2)}, u32[]{:S(2)}) collective-permute-start(f32[184,256]{1,0:T(8,128)S(1)} %collective-permute-done.first_ref.gate_ref), channel_id=1, source_target_pairs={{0,16},{1,2},{2,1},{3,19},{4,20},{5,6},{6,5},{7,23},{8,24},{9,10},... | collective-permute-start | bytes 565256 | tf_op jit(solution)/shard_map/ppermute | solution.py:577
  11.3 0.4 %own.1 = (f32[208,128]{1,0:T(8,128)S(1)}, f32[192,128]{1,0:T(8,128)S(1)}, bf16[512,384]{1,0:T(8,128)(2,1)S(1)}, bf16[512,256]{1,0:T(8,128)(2,1)S(1)}, bf16[512,3...) custom-call(f32[128,256]{1,0:T(8,128)S(1)} %get-tuple-element.36.own_q_ref, f32[128,256]{1,0:T(8,128)S(1)} %get-tuple-element.37.own_k_ref, ...), custom_call_target="tpu_custom_call" | custom-call | flops 1000000000 | bytes 3000000 | tf_op jit(solution)/shard_map/own/pallas_call | solution.py:584
  11.7 0.0 collective-permute-done.2.rest_ref
  11.7 0.0 collective-permute-done.1.second_ref
  11.7 0.1 sort.1
  11.8 1.8 %collective-permute-start.6 = (f32[296,256]{1,0:T(8,128)S(1)}, f32[296,256]{1,0:T(8,128)S(1)}, u32[]{:S(2)}, u32[]{:S(2)}) collective-permute-start(f32[296,256]{1,0:T(8,128)S(1)} %get-tuple-element.47), channel_id=1, source_target_pairs={{0,1},{1,0},{2,3},{3,2},{4,5},{5,4},{6,7},{7,6},{8,9},{9,8},{10,11... | collective-permute-start | bytes 909320 | tf_op jit(solution)/shard_map/ppermute | solution.py:594
  13.6 0.1 collective-permute-start.5
  13.7 0.0 collective-permute-done.3.odd_rest_ref
  13.7 0.4 %middle.1 = (bf16[384,384]{1,0:T(8,128)(2,1)S(1)}, bf16[384,256]{1,0:T(8,128)(2,1)S(1)}, bf16[128,384]{1,0:T(8,128)(2,1)S(1)}, bf16[128,256]{1,0:T(8,128)(2,1)S(...) custom-call(f32[184,256]{1,0:T(8,128)S(1)} %get-tuple-element.43.cor, ...), custom_call_target="tpu_custom_call" | custom-call | flops 1000000000 | bytes 3000000 | tf_op jit(solution)/shard_map/middle/pallas_call | solution.py:595
  14.1 1.2 %collective-permute-done.4.message_ref = f32[184,256]{1,0:T(8,128)S(1)} collective-permute-done((f32[184,256]{1,0:T(8,128)S(1)}, f32[184,256]{1,0:T(8,128)S(1)}, u32[]{:S(2)}, u32[]{:S(2)}) %collective-permute-start.4) | collective-permute-done | bytes 188448 | tf_op jit(solution)/shard_map/ppermute | solution.py:577
  15.3 0.0 collective-permute-done.5.even_ref
  15.3 0.0 collective-permute-done.6.mate_ref
  15.3 1.4 %even_set.1 = (f32[128,256]{1,0:T(8,128)S(1)}, f32[128,256]{1,0:T(8,128)S(1)}, f32[128,256]{1,0:T(8,128)S(1)}) custom-call(f32[128,256]{1,0:T(8,128)S(1)} %get-tuple-element.36.own_q_ref, f32[128,256]{1,0:T(8,128)S(1)} %get-tuple-element.37.own_k_ref, f32[128,256]{1,0:T(8,128)S(1)} %get-tuple-element.38.own_c_ref, ...), custom_call_target="tpu_custom_call" | custom-call | tf_op jit(solution)/shard_map/even_set/pallas_call | solution.py:606
  16.7 1.8 %odd_set.1 = (f32[128,256]{1,0:T(8,128)}, f32[128,256]{1,0:T(8,128)}, f32[128,256]{1,0:T(8,128)}) custom-call(f32[128,256]{1,0:T(8,128)S(1)} %get-tuple-element.36.own_q_ref, f32[128,256]{1,0:T(8,128)S(1)} %get-tuple-element.37.own_k_ref, f32[128,256]{1,0:T(8,128)S(1)} %get-tuple-element.38.own_c_ref, f32[184,256]{1,0:T(8,128)S(1)} %get-tuple-element.43.corner_ref, ...), custom_call_target="tpu_custom_call" | custom-call | tf_op jit(solution)/shard_map/odd_set/pallas_call | solution.py:614
  (2 shorter events, 0.0 us)
Async XLA Ops:
  1.8 7.7 %collective-permute-start = (f32[184,256]{1,0:T(8,128)S(1)}, f32[184,256]{1,0:T(8,128)S(1)}, u32[]{:S(2)}, u32[]{:S(2)}) collective-permute-start(f32[184,256]{1,0:T(8,128)S(1)} %get-tuple-element.39), channel_id=1, source_target_pairs={{0,16},{1,17},{2,18},{3,4},{4,3},{5,21},{6,22},{7,8},{8,7},{9,25},... | collective-permute-start | bytes 565256 | tf_op jit(solution)/shard_map/ppermute | solution.py:571
  4.8 6.8 %collective-permute-start.1 = (f32[184,256]{1,0:T(8,128)S(1)}, f32[184,256]{1,0:T(8,128)S(1)}, u32[]{:S(2)}, u32[]{:S(2)}) collective-permute-start(f32[184,256]{1,0:T(8,128)S(1)} %get-tuple-element.39), channel_id=1, source_target_pairs={{0,0},{1,2},{2,1},{3,19},{4,20},{5,6},{6,5},{7,23},{8,24},{9,10},{... | collective-permute-start | bytes 565256 | tf_op jit(solution)/shard_map/ppermute | solution.py:572
  5.8 5.9 %collective-permute-start.2 = (f32[112,256]{1,0:T(8,128)S(1)}, f32[112,256]{1,0:T(8,128)S(1)}, u32[]{:S(2)}, u32[]{:S(2)}) collective-permute-start(f32[112,256]{1,0:T(8,128)S(1)} %get-tuple-element.40), channel_id=1, source_target_pairs={{0,16},{16,0},{1,17},{17,1},{2,18},{18,2},{3,19},{19,3},{4,20},{20... | collective-permute-start | bytes 344072 | tf_op jit(solution)/shard_map/ppermute | solution.py:573
  5.9 7.8 %collective-permute-start.3 = (f32[112,256]{1,0:T(8,128)S(1)}, f32[112,256]{1,0:T(8,128)S(1)}, u32[]{:S(2)}, u32[]{:S(2)}) collective-permute-start(f32[112,256]{1,0:T(8,128)S(1)} %get-tuple-element.45), channel_id=1, source_target_pairs={{0,16},{1,2},{2,1},{3,4},{4,3},{5,6},{6,5},{7,8},{8,7},{9,10},{10,... | collective-permute-start | bytes 344072 | tf_op jit(solution)/shard_map/ppermute | solution.py:574
  9.6 5.7 %collective-permute-start.4 = (f32[184,256]{1,0:T(8,128)S(1)}, f32[184,256]{1,0:T(8,128)S(1)}, u32[]{:S(2)}, u32[]{:S(2)}) collective-permute-start(f32[184,256]{1,0:T(8,128)S(1)} %collective-permute-done.first_ref.gate_ref), channel_id=1, source_target_pairs={{0,16},{1,2},{2,1},{3,19},{4,20},{5,6},{6,5},{7,23},{8,24},{9,10},... | collective-permute-start | bytes 565256 | tf_op jit(solution)/shard_map/ppermute | solution.py:577
  11.8 3.5 %collective-permute-start.6 = (f32[296,256]{1,0:T(8,128)S(1)}, f32[296,256]{1,0:T(8,128)S(1)}, u32[]{:S(2)}, u32[]{:S(2)}) collective-permute-start(f32[296,256]{1,0:T(8,128)S(1)} %get-tuple-element.47), channel_id=1, source_target_pairs={{0,1},{1,0},{2,3},{3,2},{4,5},{5,4},{6,7},{7,6},{8,9},{9,8},{10,11... | collective-permute-start | bytes 909320 | tf_op jit(solution)/shard_map/ppermute | solution.py:594
  13.6 1.7 %collective-permute-start.5 = (f32[288,256]{1,0:T(8,128)S(1)}, f32[288,256]{1,0:T(8,128)S(1)}, u32[]{:S(2)}, u32[]{:S(2)}) collective-permute-start(f32[288,256]{1,0:T(8,128)S(1)} %release.1), channel_id=1, source_target_pairs={{0,1},{1,0},{2,3},{3,2},{4,5},{5,4},{6,7},{7,6},{8,9},{9,8},{10,11... | collective-permute-start | bytes 884744 | tf_op jit(solution)/shard_map/ppermute | solution.py:576

commit v3 on v2

--- a/solution.py
+++ b/solution.py
@@ -295,26 +295,28 @@
     return jnp.concatenate(out, axis=1)
 
 
-def attend(work, bias_ref, own_tokens, own_keys, inner):
+def attend(work):
     scores, dprobs = [], []
-    for key_l, value_l, query_r, cot_r, _, _, _ in work:
+    for key_l, value_l, query_r, cot_r, *_, bias_ref, _, _, _ in work:
         for head in range(HEADS):
             scores.append(dot_nt(key_l[head], query_r[head]) + bias_ref[...])
             dprobs.append(dot_nt(value_l[head], cot_r[head]))
     prob_rows, ds_rows, ds_cols = [], [], []
-    for s, dp in zip(scores, dprobs):
-        top = jnp.maximum(jnp.max(s, axis=0, keepdims=True), -1e29)
-        e = jnp.exp(s - top)
-        inv = 1.0 / jnp.maximum(jnp.sum(e, axis=0, keepdims=True), 1e-30)
-        delta = inv * jnp.sum(e * dp, axis=0, keepdims=True)
-        prob_rows.append(e[0:own_keys] * inv)
-        ds = [e[part] * inv * (dp[part] - delta) for part in inner]
-        ds_rows.append(ds[0][0:own_keys])
-        ds = jnp.concatenate(ds, axis=0) if len(ds) > 1 else ds[0]
-        ds_cols.append(ds[:, 0:own_tokens].T)
+    for item, (*_, own_tokens, own_keys, inner) in enumerate(work):
+        for head in range(HEADS):
+            s, dp = scores[HEADS * item + head], dprobs[HEADS * item + head]
+            top = jnp.maximum(jnp.max(s, axis=0, keepdims=True), -1e29)
+            e = jnp.exp(s - top)
+            inv = 1.0 / jnp.maximum(jnp.sum(e, axis=0, keepdims=True), 1e-30)
+            delta = inv * jnp.sum(e * dp, axis=0, keepdims=True)
+            prob_rows.append(e[0:own_keys] * inv)
+            ds = [e[part] * inv * (dp[part] - delta) for part in inner]
+            ds_rows.append(ds[0][0:own_keys])
+            ds = jnp.concatenate(ds, axis=0) if len(ds) > 1 else ds[0]
+            ds_cols.append(ds[:, 0:own_tokens].T)
     out = []
-    for image, (_, _, _, _, key, query, cot) in enumerate(work):
-        here = slice(HEADS * image, HEADS * image + HEADS)
+    for item, (_, _, _, _, key, query, cot, *_) in enumerate(work):
+        here = slice(HEADS * item, HEADS * item + HEADS)
         out.append((
             heads_product(ds_cols[here], key) * 0.125,
             heads_product(ds_rows[here], query),
@@ -421,8 +423,8 @@
             keep(odd_to_ref, image, stacked(x * scale, False, parts))
 
 
-def even_kernel(own_q_ref, own_k_ref, own_c_ref, corner_ref, rest_ref, even_ref, mate_ref, bias_ref,
-                k0_ref, v0_ref, q0_ref, c0_ref, k1_ref, v1_ref, q1_ref, c1_ref, dq_ref, dk_ref, dv_ref):
+def even_work(own_q_ref, own_k_ref, own_c_ref, corner_ref, rest_ref, even_ref, mate_ref, bias_ref,
+                k0_ref, v0_ref, q0_ref, c0_ref, k1_ref, v1_ref, q1_ref, c1_ref):
     work = []
     for image in range(2):
 
@@ -454,13 +456,9 @@
             jnp.concatenate(key, axis=0),
             jnp.concatenate([jnp.concatenate(query, axis=0) * 0.125, late_q], axis=0),
             jnp.concatenate(cot + [late_c], axis=0),
+            bias_ref, 64, 64, (slice(0, 88), slice(112, 136), slice(160, 184)),
         ))
-    parts = attend(work, bias_ref, 64, 64, (slice(0, 88), slice(112, 136), slice(160, 184)))
-    for image, (dq, dk, dv) in enumerate(parts):
-        here = slice(64 * image, 64 * image + 64)
-        dq_ref[here, :] = dq
-        dk_ref[here, :] = dk
-        dv_ref[here, :] = dv
+    return work
 
 
 def sort_kernel(cols, first_ref, second_ref, rest_ref, gate_ref, ha_ref, odd_ref, mate_ref):
@@ -481,10 +479,7 @@
     return jnp.logical_and(((w + 1) >> 1) % 2 == 0, jnp.logical_and(w > 0, w < cols - 1))
 
 
-def odd_kernel(own_q_ref, own_k_ref, own_c_ref, corner_ref, odd_ref, odd_rest_ref, far_ref, even_dq_ref, even_dk_ref,
-               even_dv_ref, bias_ref, k0_ref, v0_ref, q0_ref, c0_ref, k1_ref, v1_ref, q1_ref, c1_ref,
-               dq_ref, dk_ref, dv_ref, split_ref):
-    p = lax.axis_index("wa") % 2
+def odd_work(own_q_ref, own_k_ref, own_c_ref, corner_ref, odd_ref, odd_rest_ref, far_ref, bias_ref, k0_ref, v0_ref, q0_ref, c0_ref, k1_ref, v1_ref, q1_ref, c1_ref):
     work = []
     for image in range(2):
 
@@ -509,15 +504,28 @@
             jnp.concatenate(key, axis=0),
             jnp.concatenate([jnp.concatenate(query, axis=0) * 0.125, late_q], axis=0),
             jnp.concatenate(cot + [late_c], axis=0),
+            bias_ref, 24, 48, (slice(0, 72), slice(96, 120), slice(144, 160)),
         ))
-    parts = attend(work, bias_ref, 24, 48, (slice(0, 72), slice(96, 120), slice(144, 160)))
-    for image, (dq, dk, dv) in enumerate(parts):
-        here = slice(64 * image, 64 * image + 64)
+    return work
+
+
+def last_kernel(own_q_ref, own_k_ref, own_c_ref, corner_ref, rest_ref, even_ref, mate_ref, odd_ref, odd_rest_ref, far_ref,
+                even_bias_ref, odd_bias_ref, k0_ref, v0_ref, q0_ref, c0_ref, k1_ref, v1_ref, q1_ref, c1_ref,
+                k2_ref, v2_ref, q2_ref, c2_ref, dq_ref, dk_ref, dv_ref, split_ref):
+    p = lax.axis_index("wa") % 2
+    own = (own_q_ref, own_k_ref, own_c_ref)
+    kept = (k0_ref, v0_ref, q0_ref, c0_ref)
+    work = even_work(*own, corner_ref, rest_ref, even_ref, mate_ref, even_bias_ref, *kept, k1_ref, v1_ref, q1_ref, c1_ref)
+    work += odd_work(*own, corner_ref, odd_ref, odd_rest_ref, far_ref, odd_bias_ref, *kept, k2_ref, v2_ref, q2_ref, c2_ref)
+    parts = attend(work)
+    for image in range(2):
+        even_dq, even_dk, even_dv = parts[image]
+        dq, dk, dv = parts[2 + image]
         none = jnp.zeros((16, 256), F32)
         results = (
-            jnp.concatenate([dq, jnp.zeros((40, 256), F32)], axis=0) + even_dq_ref[here, :],
-            jnp.concatenate([dk, none], axis=0) + even_dk_ref[here, :],
-            jnp.concatenate([dv, none], axis=0) + even_dv_ref[here, :],
+            jnp.concatenate([dq, jnp.zeros((40, 256), F32)], axis=0) + even_dq,
+            jnp.concatenate([dk, none], axis=0) + even_dk,
+            jnp.concatenate([dv, none], axis=0) + even_dv,
         )
         for index, x in enumerate(results):
             for slot in range(8):
@@ -530,10 +538,10 @@
 
 
 SMALL = pltpu.CompilerParams(vmem_limit_bytes=6 * 1024 * 1024)
-OWN_US = 1
+LARGE = pltpu.CompilerParams(vmem_limit_bytes=12 * 1024 * 1024)
+OWN_US = 0
 PREP_US = 1
 FAR_US = 2
-EVEN_US = 0
 
 
 def cost(micros):
@@ -603,21 +611,15 @@
         far = pl.pallas_call(
             release_kernel, out_shape=vmem(184), cost_estimate=cost(FAR_US), name="arrive_far", compiler_params=SMALL,
         )(held(far), held(first))
-    even_part = pl.pallas_call(
-        even_kernel,
-        out_shape=(vmem(128), vmem(128), vmem(128)),
-        compiler_params=SMALL,
-        cost_estimate=cost(EVEN_US),
-        name="even_set",
-    )(*[held(x) for x in (own_q, own_k, own_c, corner, rest, even, mate, even_bias, *own_stacks, *middle[0:4])])
     out = jax.ShapeDtypeStruct((128, 256), F32)
     grads = pl.pallas_call(
-        odd_kernel,
+        last_kernel,
         out_shape=(out, out, out),
         scratch_shapes=[pltpu.VMEM((6, 128, 128), F32)],
-        compiler_params=SMALL,
-        name="odd_set",
-    )(*[held(x) for x in (own_q, own_k, own_c, corner, odd, odd_rest, far, *even_part, odd_bias, *own_stacks, *middle[4:8])])
+        compiler_params=LARGE,
+        name="attend",
+    )(*[held(x) for x in (own_q, own_k, own_c, corner, rest, even, mate, odd, odd_rest, far, even_bias, odd_bias,
+                          *own_stacks, *middle)])
     return tuple(g.reshape(shape) for g in grads)
 
 

time: 18.6 us -> 18.3 us (0.984)
  Pallas kernels: 5.55 us -> 5.21 us
    pallas_call x2 -> x1, Pallas kernels: 3.17 us -> 2.83 us  [per_device(): pl.pallas_call(last_kernel, out_shape=(out, out, out), scratch_shapes=[pl...]
where the time goes in v3:
time: 18.3 us; the launch traced here: 18.1 us
  starting transfers between devices  9.37 us (51%)
  Pallas kernels  5.21 us (28%)
  waiting for transfers between devices  2.86 us (16%)
  between operations  0.71 us (4%)
    ppermute x1, starting transfers between devices, per_device(): first = lax.ppermute(to_corner, both, first_pairs)  3 us
    pallas_call x1, Pallas kernels, per_device(): pl.pallas_call(last_kernel, out_shape=(out, out, out), scratch_shapes=[pl...  2.83 us
    ppermute x1, starting transfers between devices, per_device(): odd_rest = lax.ppermute(to_odd_rest, both, odd_pairs)  2 us
    ppermute x1, starting transfers between devices, per_device(): mate = lax.ppermute(to_mate, 'wa', even_pairs)  1.79 us
    ppermute x1, starting transfers between devices, per_device(): far = lax.ppermute(first, both, far_pairs)  1.74 us
    ppermute x1, waiting for transfers between devices, per_device(): first = lax.ppermute(to_corner, both, first_pairs)  1.67 us
    pallas_call x1, Pallas kernels, per_device(): pl.pallas_call(corner_kernel, out_shape=(vmem(184), pltpu.VMEM((8, 128, 1...  1.21 us
    ppermute x1, waiting for transfers between devices, per_device(): far = lax.ppermute(first, both, far_pairs)  1.18 us
  transfers between devices with their start and end apart: 7, of which 2 were waited for; matrix products, arithmetic and copies ran while one was open for 0% of the time, Pallas kernels for 6%

profile of v3, /device:TPU:0, one launch (start us, length us, event | category | flops | bytes accessed | tf_op | source)
XLA Modules:
  0.0 18.1 jit_solution(16632148885511620753)
XLA Ops:
  0.6 1.2 %corner.1 = (f32[184,256]{1,0:T(8,128)S(1)}, f32[8,128,128]{2,1,0:T(8,128)S(1)}) custom-call(f32[128,256]{1,0:T(8,128)} %bitcast.7, f32[128,256]{1,0:T(8,128)} %bitcast.8, f32[128,256]{1,0:T(8,128)} %bitcast.9, f32[128,256]{1,0:T(8,128)} %bitcast.10), custom_call_target="tpu_custom_call" | custom-call | tf_op jit(solution)/shard_map/corner/pallas_call | solution.py:555
  1.8 3.0 %collective-permute-start = (f32[184,256]{1,0:T(8,128)S(1)}, f32[184,256]{1,0:T(8,128)S(1)}, u32[]{:S(2)}, u32[]{:S(2)}) collective-permute-start(f32[184,256]{1,0:T(8,128)S(1)} %get-tuple-element.36), channel_id=1, source_target_pairs={{0,16},{1,17},{2,18},{3,4},{4,3},{5,21},{6,22},{7,8},{8,7},{9,25},... | collective-permute-start | bytes 565256 | tf_op jit(solution)/shard_map/ppermute | solution.py:579
  4.8 0.7 %collective-permute-start.1 = (f32[184,256]{1,0:T(8,128)S(1)}, f32[184,256]{1,0:T(8,128)S(1)}, u32[]{:S(2)}, u32[]{:S(2)}) collective-permute-start(f32[184,256]{1,0:T(8,128)S(1)} %get-tuple-element.36), channel_id=1, source_target_pairs={{0,0},{1,2},{2,1},{3,19},{4,20},{5,6},{6,5},{7,23},{8,24},{9,10},{... | collective-permute-start | bytes 565256 | tf_op jit(solution)/shard_map/ppermute | solution.py:580
  5.5 0.3 %pack.1 = (f32[112,256]{1,0:T(8,128)S(1)}, f32[112,256]{1,0:T(8,128)S(1)}, f32[288,256]{1,0:T(8,128)S(1)}, f32[128,256]{1,0:T(8,128)S(1)}, f32[128,256]{1,0:T(8,...) custom-call(f32[8,128,128]{2,1,0:T(8,128)S(1)} %get-tuple-element.32.split_ref), custom_call_target="tpu_custom_call" | custom-call | tf_op jit(solution)/shard_map/pack/pallas_call | solution.py:558
  5.8 0.1 collective-permute-start.2
  5.9 2.0 %collective-permute-start.5 = (f32[112,256]{1,0:T(8,128)S(1)}, f32[112,256]{1,0:T(8,128)S(1)}, u32[]{:S(2)}, u32[]{:S(2)}) collective-permute-start(f32[112,256]{1,0:T(8,128)S(1)} %get-tuple-element.44), channel_id=1, source_target_pairs={{0,16},{1,2},{2,1},{3,4},{4,3},{5,6},{6,5},{7,8},{8,7},{9,10},{10,... | collective-permute-start | bytes 344072 | tf_op jit(solution)/shard_map/ppermute | solution.py:582
  7.9 1.7 %collective-permute-done.first_ref.gate_ref = f32[184,256]{1,0:T(8,128)S(1)} collective-permute-done((f32[184,256]{1,0:T(8,128)S(1)}, f32[184,256]{1,0:T(8,128)S(1)}, u32[]{:S(2)}, u32[]{:S(2)}) %collective-permute-start) | collective-permute-done | bytes 188448 | tf_op jit(solution)/shard_map/ppermute | solution.py:579
  9.6 1.7 %collective-permute-start.6 = (f32[184,256]{1,0:T(8,128)S(1)}, f32[184,256]{1,0:T(8,128)S(1)}, u32[]{:S(2)}, u32[]{:S(2)}) collective-permute-start(f32[184,256]{1,0:T(8,128)S(1)} %collective-permute-done.first_ref.gate_ref), channel_id=1, source_target_pairs={{0,16},{1,2},{2,1},{3,19},{4,20},{5,6},{6,5},{7,23},{8,24},{9,10},... | collective-permute-start | bytes 565256 | tf_op jit(solution)/shard_map/ppermute | solution.py:585
  11.3 0.4 %own.1 = (f32[208,128]{1,0:T(8,128)S(1)}, f32[192,128]{1,0:T(8,128)S(1)}, bf16[512,384]{1,0:T(8,128)(2,1)S(1)}, bf16[512,256]{1,0:T(8,128)(2,1)S(1)}, bf16[512,3...) custom-call(f32[128,256]{1,0:T(8,128)S(1)} %get-tuple-element.33.own_q_ref, f32[128,256]{1,0:T(8,128)S(1)} %get-tuple-element.34.own_k_ref, ...), custom_call_target="tpu_custom_call" | custom-call | tf_op jit(solution)/shard_map/own/pallas_call | solution.py:592
  11.7 0.0 collective-permute-done.2.rest_ref
  11.7 0.0 collective-permute-done.1.second_ref
  11.7 0.1 sort.1
  11.8 1.8 %collective-permute-start.4 = (f32[296,256]{1,0:T(8,128)S(1)}, f32[296,256]{1,0:T(8,128)S(1)}, u32[]{:S(2)}, u32[]{:S(2)}) collective-permute-start(f32[296,256]{1,0:T(8,128)S(1)} %get-tuple-element.42), channel_id=1, source_target_pairs={{0,1},{1,0},{2,3},{3,2},{4,5},{5,4},{6,7},{7,6},{8,9},{9,8},{10,11... | collective-permute-start | bytes 909320 | tf_op jit(solution)/shard_map/ppermute | solution.py:602
  13.6 0.1 collective-permute-start.3
  13.7 0.0 collective-permute-done.5.odd_rest_ref
  13.7 0.4 %middle.1 = (bf16[384,384]{1,0:T(8,128)(2,1)S(1)}, bf16[384,256]{1,0:T(8,128)(2,1)S(1)}, bf16[128,384]{1,0:T(8,128)(2,1)S(1)}, bf16[128,256]{1,0:T(8,128)(2,1)S(...) custom-call(f32[184,256]{1,0:T(8,128)S(1)} %get-tuple-element.40.cor, ...), custom_call_target="tpu_custom_call" | custom-call | flops 1000000000 | bytes 3000000 | tf_op jit(solution)/shard_map/middle/pallas_call | solution.py:603
  14.1 1.2 %collective-permute-done.6.message_ref = f32[184,256]{1,0:T(8,128)S(1)} collective-permute-done((f32[184,256]{1,0:T(8,128)S(1)}, f32[184,256]{1,0:T(8,128)S(1)}, u32[]{:S(2)}, u32[]{:S(2)}) %collective-permute-start.6) | collective-permute-done | bytes 188448 | tf_op jit(solution)/shard_map/ppermute | solution.py:585
  15.3 0.0 collective-permute-done.3.even_ref
  15.3 0.0 collective-permute-done.4.mate_ref
  15.3 2.8 %attend.1 = (f32[128,256]{1,0:T(8,128)}, f32[128,256]{1,0:T(8,128)}, f32[128,256]{1,0:T(8,128)}) custom-call(f32[128,256]{1,0:T(8,128)S(1)} %get-tuple-element.33.own_q_ref, f32[128,256]{1,0:T(8,128)S(1)} %get-tuple-element.34.own_k_ref, f32[128,256]{1,0:T(8,128)S(1)} %get-tuple-element.35.own_c_ref, f32[184,256]{1,0:T(8,128)S(1)} %get-tuple-element.40.corner_ref, ...), custom_call_target="tpu_custom_call" | custom-call | tf_op jit(solution)/shard_map/attend/pallas_call | solution.py:615
  (2 shorter events, 0.0 us)
Async XLA Ops:
  1.8 7.7 %collective-permute-start = (f32[184,256]{1,0:T(8,128)S(1)}, f32[184,256]{1,0:T(8,128)S(1)}, u32[]{:S(2)}, u32[]{:S(2)}) collective-permute-start(f32[184,256]{1,0:T(8,128)S(1)} %get-tuple-element.36), channel_id=1, source_target_pairs={{0,16},{1,17},{2,18},{3,4},{4,3},{5,21},{6,22},{7,8},{8,7},{9,25},... | collective-permute-start | bytes 565256 | tf_op jit(solution)/shard_map/ppermute | solution.py:579
  4.8 6.8 %collective-permute-start.1 = (f32[184,256]{1,0:T(8,128)S(1)}, f32[184,256]{1,0:T(8,128)S(1)}, u32[]{:S(2)}, u32[]{:S(2)}) collective-permute-start(f32[184,256]{1,0:T(8,128)S(1)} %get-tuple-element.36), channel_id=1, source_target_pairs={{0,0},{1,2},{2,1},{3,19},{4,20},{5,6},{6,5},{7,23},{8,24},{9,10},{... | collective-permute-start | bytes 565256 | tf_op jit(solution)/shard_map/ppermute | solution.py:580
  5.8 5.9 %collective-permute-start.2 = (f32[112,256]{1,0:T(8,128)S(1)}, f32[112,256]{1,0:T(8,128)S(1)}, u32[]{:S(2)}, u32[]{:S(2)}) collective-permute-start(f32[112,256]{1,0:T(8,128)S(1)} %get-tuple-element.37), channel_id=1, source_target_pairs={{0,16},{16,0},{1,17},{17,1},{2,18},{18,2},{3,19},{19,3},{4,20},{20... | collective-permute-start | bytes 344072 | tf_op jit(solution)/shard_map/ppermute | solution.py:581
  5.9 7.8 %collective-permute-start.5 = (f32[112,256]{1,0:T(8,128)S(1)}, f32[112,256]{1,0:T(8,128)S(1)}, u32[]{:S(2)}, u32[]{:S(2)}) collective-permute-start(f32[112,256]{1,0:T(8,128)S(1)} %get-tuple-element.44), channel_id=1, source_target_pairs={{0,16},{1,2},{2,1},{3,4},{4,3},{5,6},{6,5},{7,8},{8,7},{9,10},{10,... | collective-permute-start | bytes 344072 | tf_op jit(solution)/shard_map/ppermute | solution.py:582
  9.6 5.7 %collective-permute-start.6 = (f32[184,256]{1,0:T(8,128)S(1)}, f32[184,256]{1,0:T(8,128)S(1)}, u32[]{:S(2)}, u32[]{:S(2)}) collective-permute-start(f32[184,256]{1,0:T(8,128)S(1)} %collective-permute-done.first_ref.gate_ref), channel_id=1, source_target_pairs={{0,16},{1,2},{2,1},{3,19},{4,20},{5,6},{6,5},{7,23},{8,24},{9,10},... | collective-permute-start | bytes 565256 | tf_op jit(solution)/shard_map/ppermute | solution.py:585
  11.8 3.5 %collective-permute-start.4 = (f32[296,256]{1,0:T(8,128)S(1)}, f32[296,256]{1,0:T(8,128)S(1)}, u32[]{:S(2)}, u32[]{:S(2)}) collective-permute-start(f32[296,256]{1,0:T(8,128)S(1)} %get-tuple-element.42), channel_id=1, source_target_pairs={{0,1},{1,0},{2,3},{3,2},{4,5},{5,4},{6,7},{7,6},{8,9},{9,8},{10,11... | collective-permute-start | bytes 909320 | tf_op jit(solution)/shard_map/ppermute | solution.py:602
  13.6 1.7 %collective-permute-start.3 = (f32[288,256]{1,0:T(8,128)S(1)}, f32[288,256]{1,0:T(8,128)S(1)}, u32[]{:S(2)}, u32[]{:S(2)}) collective-permute-start(f32[288,256]{1,0:T(8,128)S(1)} %release.1), channel_id=1, source_target_pairs={{0,1},{1,0},{2,3},{3,2},{4,5},{5,4},{6,7},{7,6},{8,9},{9,8},{10,11... | collective-permute-start | bytes 884744 | tf_op jit(solution)/shard_map/ppermute | solution.py:584

commit v4 on v3

--- a/solution.py
+++ b/solution.py
@@ -37,6 +37,8 @@
 
 
 WIDE = (True, True, False, False)
+
+SPLIT = 136
 
 
 def corner_kernel(k_ref, v_ref, q_ref, c_ref, corner_ref, split_ref):
@@ -47,7 +49,7 @@
     col = pack_reader(split_ref)
     for index, ref in enumerate((k_ref, v_ref, q_ref, c_ref)):
         for half in range(2):
-            split_ref[2 * index + half] = ref[:, 128 * half : 128 * half + 128]
+            split_ref[2 * index + half, 0:128, :] = ref[:, 128 * half : 128 * half + 128]
     for image in range(2):
         at = 90 * image
         for index, wide in enumerate(WIDE):
@@ -125,6 +127,11 @@
     def ha_out(self, i):
         j = third(i)
         return self.row_out + (i - 3 * j), slot_column(self.p, j)
+
+    def mate_in(self, i):
+        j = third(i)
+        slot = jnp.where(j < 5, j + 3, j - 5)
+        return self.row_in + (i - 3 * j), self.even_all + slot_column(1 - self.p, slot)
 
     def deven_in(self, i):
         j = third(i)
@@ -284,13 +291,9 @@
         lanes = slice(128 * pair, 128 * pair + 128)
         left_hi, left_lo = two(jnp.concatenate(per_head[2 * pair : 2 * pair + 2], axis=0))
         both = jnp.concatenate([hi[:, lanes], lo[:, lanes]], axis=1)
-        if depth == 128:
-            below = jnp.concatenate([hi[:, lanes], jnp.zeros((depth, 128), BF)], axis=1)
-            full = dot_nn(jnp.concatenate([left_hi, left_lo], axis=1), jnp.concatenate([both, below], axis=0))
-            full = full[:, 0:128] + full[:, 128:256]
-        else:
-            full = dot_nn(left_hi, both)
-            full = full[:, 0:128] + (full[:, 128:256] + dot_nn(left_lo, hi[:, lanes]))
+        below = jnp.concatenate([hi[:, lanes], jnp.zeros((depth, 128), BF)], axis=1)
+        full = dot_nn(jnp.concatenate([left_hi, left_lo], axis=1), jnp.concatenate([both, below], axis=0))
+        full = full[:, 0:128] + full[:, 128:256]
         out.append(jnp.where(low, full[0:rows], full[rows : 2 * rows]))
     return jnp.concatenate(out, axis=1)
 
@@ -312,7 +315,8 @@
             prob_rows.append(e[0:own_keys] * inv)
             ds = [e[part] * inv * (dp[part] - delta) for part in inner]
             ds_rows.append(ds[0][0:own_keys])
-            ds = jnp.concatenate(ds, axis=0) if len(ds) > 1 else ds[0]
+            short = 128 - sum(x.shape[0] for x in ds)
+            ds = jnp.concatenate(ds + [jnp.zeros((short, 128), F32)] * (short > 0), axis=0)
             ds_cols.append(ds[:, 0:own_tokens].T)
     out = []
     for item, (_, _, _, _, key, query, cot, *_) in enumerate(work):
@@ -363,7 +367,7 @@
     write_bias(
         even_bias_ref,
         ((at.own, 64, 64), (at.ha_in, 24, 24), (at.ha_out, 24, 24), (at.even_inner, 24, 24), (at.even_outer, 24, 24),
-         (at.deven_in, 24, 24), (at.deven_out, 24, 24)),
+         (at.mate_in, 24, 24), (at.deven_out, 24, 24)),
         ((None, 0, 24), (lambda i: at.own(i, 3), 40, 40), (lambda i: at.ha_in(i, 3), 15, 16), (at.even_inner, 24, 24),
          (at.deven_in, 24, 24)),
     )
@@ -429,7 +433,9 @@
     for image in range(2):
 
         def mate_inner(field):
-            return rows(mate_ref, 90 * image + CORNER[field], 18) + rows(mate_ref, 184 + 54 * image + REST[field], 6)
+            corner = 90 * image + CORNER[field]
+            out = rows(mate_ref, corner + 9, 9) + rows(mate_ref, 184 + 54 * image + REST[field], 6)
+            return out + rows(mate_ref, corner, 9)
 
         def late_keys(field):
             even = 144 * image + SIDE[field]
@@ -445,7 +451,7 @@
 
         late_q, late_c = late_tokens(2) * 0.125, late_tokens(3)
         key = rows(own_k_ref, 64 * image, 64) + ha_inner(image, corner_ref, rest_ref, 0)
-        key += rows(even_ref, 144 * image, 24) + mate_inner(0)
+        key += rows(even_ref, 144 * image, 24) + [jnp.concatenate(mate_inner(0), axis=0)[0:16]]
         query = rows(own_q_ref, 64 * image, 64) + rows(rest_ref, 54 * image + REST[2], 15, 1)
         cot = rows(own_c_ref, 64 * image, 64) + rows(rest_ref, 54 * image + REST[3], 15, 1)
         work.append((
@@ -456,7 +462,7 @@
             jnp.concatenate(key, axis=0),
             jnp.concatenate([jnp.concatenate(query, axis=0) * 0.125, late_q], axis=0),
             jnp.concatenate(cot + [late_c], axis=0),
-            bias_ref, 64, 64, (slice(0, 88), slice(112, 136), slice(160, 184)),
+            bias_ref, 64, 64, (slice(0, 88), slice(112, 136), slice(160, 176)),
         ))
     return work
 
@@ -534,13 +540,13 @@
                     split_ref[2 * index + half, where, :] = x[8 * slot : 8 * slot + 8, 128 * half : 128 * half + 128]
     for index, ref in enumerate((dq_ref, dk_ref, dv_ref)):
         for half in range(2):
-            ref[:, 128 * half : 128 * half + 128] = split_ref[2 * index + half]
+            ref[:, 128 * half : 128 * half + 128] = split_ref[2 * index + half, 0:128, :]
 
 
 SMALL = pltpu.CompilerParams(vmem_limit_bytes=6 * 1024 * 1024)
 LARGE = pltpu.CompilerParams(vmem_limit_bytes=12 * 1024 * 1024)
 OWN_US = 0
-PREP_US = 1
+PREP_US = 1.5
 FAR_US = 2
 
 
@@ -553,7 +559,7 @@
     cols = lax.axis_size("wa")
     flat = [x.reshape(128, 256) for x in (queries, keys, values, cotangent)]
     to_corner, split = pl.pallas_call(
-        corner_kernel, out_shape=(vmem(184), pltpu.VMEM((8, 128, 128), F32)), name="corner",
+        corner_kernel, out_shape=(vmem(184), pltpu.VMEM((8, SPLIT, 128), F32)), name="corner",
     )(flat[1], flat[2], flat[0], flat[3])
     to_rest, to_odd_rest, to_even, own_k, own_v, own_q, own_c = pl.pallas_call(
         pack_kernel, out_shape=(vmem(112), vmem(112), vmem(288)) + (vmem(128),) * 4, name="pack", compiler_params=SMALL,
@@ -615,7 +621,7 @@
     grads = pl.pallas_call(
         last_kernel,
         out_shape=(out, out, out),
-        scratch_shapes=[pltpu.VMEM((6, 128, 128), F32)],
+        scratch_shapes=[pltpu.VMEM((6, SPLIT, 128), F32)],
         compiler_params=LARGE,
         name="attend",
     )(*[held(x) for x in (own_q, own_k, own_c, corner, rest, even, mate, odd, odd_rest, far, even_bias, odd_bias,

time: 18.3 us -> 18.2 us (level)
  no operation moved by 1% of the time
where the time goes in v4:
time: 18.2 us; the launch traced here: 18.1 us
  starting transfers between devices  9.24 us (51%)
  Pallas kernels  5.15 us (28%)
  waiting for transfers between devices  2.98 us (16%)
  between operations  0.72 us (4%)
    ppermute x1, starting transfers between devices, per_device(): first = lax.ppermute(to_corner, both, first_pairs)  3 us
    pallas_call x1, Pallas kernels, per_device(): pl.pallas_call(last_kernel, out_shape=(out, out, out), scratch_shapes=[pl...  2.77 us
    ppermute x1, starting transfers between devices, per_device(): odd_rest = lax.ppermute(to_odd_rest, both, odd_pairs)  2 us
    ppermute x1, starting transfers between devices, per_device(): far = lax.ppermute(first, both, far_pairs)  1.74 us
    ppermute x1, waiting for transfers between devices, per_device(): first = lax.ppermute(to_corner, both, first_pairs)  1.67 us
    ppermute x1, starting transfers between devices, per_device(): mate = lax.ppermute(to_mate, 'wa', even_pairs)  1.67 us
    ppermute x1, waiting for transfers between devices, per_device(): far = lax.ppermute(first, both, far_pairs)  1.29 us
    pallas_call x1, Pallas kernels, per_device(): pl.pallas_call(corner_kernel, out_shape=(vmem(184), pltpu.VMEM((8, SPLIT,...  1.21 us
  transfers between devices with their start and end apart: 7, of which 2 were waited for; matrix products, arithmetic and copies ran while one was open for 0% of the time, Pallas kernels for 6%

profile of v4, /device:TPU:0, one launch (start us, length us, event | category | flops | bytes accessed | tf_op | source)
XLA Modules:
  0.0 18.1 jit_solution(55374222492009187)
XLA Ops:
  0.6 1.2 %corner.1 = (f32[184,256]{1,0:T(8,128)S(1)}, f32[8,136,128]{2,1,0:T(8,128)S(1)}) custom-call(f32[128,256]{1,0:T(8,128)} %bitcast.7, f32[128,256]{1,0:T(8,128)} %bitcast.8, f32[128,256]{1,0:T(8,128)} %bitcast.9, f32[128,256]{1,0:T(8,128)} %bitcast.10), custom_call_target="tpu_custom_call" | custom-call | tf_op jit(solution)/shard_map/corner/pallas_call | solution.py:561
  1.8 3.0 %collective-permute-start = (f32[184,256]{1,0:T(8,128)S(1)}, f32[184,256]{1,0:T(8,128)S(1)}, u32[]{:S(2)}, u32[]{:S(2)}) collective-permute-start(f32[184,256]{1,0:T(8,128)S(1)} %get-tuple-element.36), channel_id=1, source_target_pairs={{0,16},{1,17},{2,18},{3,4},{4,3},{5,21},{6,22},{7,8},{8,7},{9,25},... | collective-permute-start | bytes 565256 | tf_op jit(solution)/shard_map/ppermute | solution.py:585
  4.8 0.7 %collective-permute-start.1 = (f32[184,256]{1,0:T(8,128)S(1)}, f32[184,256]{1,0:T(8,128)S(1)}, u32[]{:S(2)}, u32[]{:S(2)}) collective-permute-start(f32[184,256]{1,0:T(8,128)S(1)} %get-tuple-element.36), channel_id=1, source_target_pairs={{0,0},{1,2},{2,1},{3,19},{4,20},{5,6},{6,5},{7,23},{8,24},{9,10},{... | collective-permute-start | bytes 565256 | tf_op jit(solution)/shard_map/ppermute | solution.py:586
  5.5 0.3 %pack.1 = (f32[112,256]{1,0:T(8,128)S(1)}, f32[112,256]{1,0:T(8,128)S(1)}, f32[288,256]{1,0:T(8,128)S(1)}, f32[128,256]{1,0:T(8,128)S(1)}, f32[128,256]{1,0:T(8,...) custom-call(f32[8,136,128]{2,1,0:T(8,128)S(1)} %get-tuple-element.32.split_ref), custom_call_target="tpu_custom_call" | custom-call | tf_op jit(solution)/shard_map/pack/pallas_call | solution.py:564
  5.8 0.1 collective-permute-start.2
  5.9 2.0 %collective-permute-start.5 = (f32[112,256]{1,0:T(8,128)S(1)}, f32[112,256]{1,0:T(8,128)S(1)}, u32[]{:S(2)}, u32[]{:S(2)}) collective-permute-start(f32[112,256]{1,0:T(8,128)S(1)} %get-tuple-element.44), channel_id=1, source_target_pairs={{0,16},{1,2},{2,1},{3,4},{4,3},{5,6},{6,5},{7,8},{8,7},{9,10},{10,... | collective-permute-start | bytes 344072 | tf_op jit(solution)/shard_map/ppermute | solution.py:588
  7.9 1.7 %collective-permute-done.first_ref.gate_ref = f32[184,256]{1,0:T(8,128)S(1)} collective-permute-done((f32[184,256]{1,0:T(8,128)S(1)}, f32[184,256]{1,0:T(8,128)S(1)}, u32[]{:S(2)}, u32[]{:S(2)}) %collective-permute-start) | collective-permute-done | bytes 188448 | tf_op jit(solution)/shard_map/ppermute | solution.py:585
  9.6 1.7 %collective-permute-start.6 = (f32[184,256]{1,0:T(8,128)S(1)}, f32[184,256]{1,0:T(8,128)S(1)}, u32[]{:S(2)}, u32[]{:S(2)}) collective-permute-start(f32[184,256]{1,0:T(8,128)S(1)} %collective-permute-done.first_ref.gate_ref), channel_id=1, source_target_pairs={{0,16},{1,2},{2,1},{3,19},{4,20},{5,6},{6,5},{7,23},{8,24},{9,10},... | collective-permute-start | bytes 565256 | tf_op jit(solution)/shard_map/ppermute | solution.py:591
  11.3 0.4 %own.1 = (f32[208,128]{1,0:T(8,128)S(1)}, f32[192,128]{1,0:T(8,128)S(1)}, bf16[512,384]{1,0:T(8,128)(2,1)S(1)}, bf16[512,256]{1,0:T(8,128)(2,1)S(1)}, bf16[512,3...) custom-call(f32[128,256]{1,0:T(8,128)S(1)} %get-tuple-element.33.own_q_ref, f32[128,256]{1,0:T(8,128)S(1)} %get-tuple-element.34.own_k_ref, ...), custom_call_target="tpu_custom_call" | custom-call | tf_op jit(solution)/shard_map/own/pallas_call | solution.py:598
  11.7 0.1 collective-permute-start.3
  11.8 0.0 collective-permute-done.2.rest_ref
  11.8 0.0 collective-permute-done.1.second_ref
  11.8 0.1 sort.1
  11.9 1.7 %collective-permute-start.4 = (f32[296,256]{1,0:T(8,128)S(1)}, f32[296,256]{1,0:T(8,128)S(1)}, u32[]{:S(2)}, u32[]{:S(2)}) collective-permute-start(f32[296,256]{1,0:T(8,128)S(1)} %get-tuple-element.42), channel_id=1, source_target_pairs={{0,1},{1,0},{2,3},{3,2},{4,5},{5,4},{6,7},{7,6},{8,9},{9,8},{10,11... | collective-permute-start | bytes 909320 | tf_op jit(solution)/shard_map/ppermute | solution.py:608
  13.6 0.0 collective-permute-done.5.odd_rest_ref
  13.6 0.4 %middle.1 = (bf16[384,384]{1,0:T(8,128)(2,1)S(1)}, bf16[384,256]{1,0:T(8,128)(2,1)S(1)}, bf16[128,384]{1,0:T(8,128)(2,1)S(1)}, bf16[128,256]{1,0:T(8,128)(2,1)S(...) custom-call(f32[184,256]{1,0:T(8,128)S(1)} %get-tuple-element.40.cor, ...), custom_call_target="tpu_custom_call" | custom-call | flops 1500000000 | bytes 4500000 | tf_op jit(solution)/shard_map/middle/pallas_call | solution.py:609
  14.0 1.3 %collective-permute-done.6.message_ref = f32[184,256]{1,0:T(8,128)S(1)} collective-permute-done((f32[184,256]{1,0:T(8,128)S(1)}, f32[184,256]{1,0:T(8,128)S(1)}, u32[]{:S(2)}, u32[]{:S(2)}) %collective-permute-start.6) | collective-permute-done | bytes 188448 | tf_op jit(solution)/shard_map/ppermute | solution.py:591
  15.3 0.0 collective-permute-done.3.even_ref
  15.3 0.0 collective-permute-done.4.mate_ref
  15.3 2.8 %attend.1 = (f32[128,256]{1,0:T(8,128)}, f32[128,256]{1,0:T(8,128)}, f32[128,256]{1,0:T(8,128)}) custom-call(f32[128,256]{1,0:T(8,128)S(1)} %get-tuple-element.33.own_q_ref, f32[128,256]{1,0:T(8,128)S(1)} %get-tuple-element.34.own_k_ref, f32[128,256]{1,0:T(8,128)S(1)} %get-tuple-element.35.own_c_ref, f32[184,256]{1,0:T(8,128)S(1)} %get-tuple-element.40.corner_ref, ...), custom_call_target="tpu_custom_call" | custom-call | tf_op jit(solution)/shard_map/attend/pallas_call | solution.py:621
  (2 shorter events, 0.0 us)
Async XLA Ops:
  1.8 7.7 %collective-permute-start = (f32[184,256]{1,0:T(8,128)S(1)}, f32[184,256]{1,0:T(8,128)S(1)}, u32[]{:S(2)}, u32[]{:S(2)}) collective-permute-start(f32[184,256]{1,0:T(8,128)S(1)} %get-tuple-element.36), channel_id=1, source_target_pairs={{0,16},{1,17},{2,18},{3,4},{4,3},{5,21},{6,22},{7,8},{8,7},{9,25},... | collective-permute-start | bytes 565256 | tf_op jit(solution)/shard_map/ppermute | solution.py:585
  4.8 7.0 %collective-permute-start.1 = (f32[184,256]{1,0:T(8,128)S(1)}, f32[184,256]{1,0:T(8,128)S(1)}, u32[]{:S(2)}, u32[]{:S(2)}) collective-permute-start(f32[184,256]{1,0:T(8,128)S(1)} %get-tuple-element.36), channel_id=1, source_target_pairs={{0,0},{1,2},{2,1},{3,19},{4,20},{5,6},{6,5},{7,23},{8,24},{9,10},{... | collective-permute-start | bytes 565256 | tf_op jit(solution)/shard_map/ppermute | solution.py:586
  5.8 6.0 %collective-permute-start.2 = (f32[112,256]{1,0:T(8,128)S(1)}, f32[112,256]{1,0:T(8,128)S(1)}, u32[]{:S(2)}, u32[]{:S(2)}) collective-permute-start(f32[112,256]{1,0:T(8,128)S(1)} %get-tuple-element.37), channel_id=1, source_target_pairs={{0,16},{16,0},{1,17},{17,1},{2,18},{18,2},{3,19},{19,3},{4,20},{20... | collective-permute-start | bytes 344072 | tf_op jit(solution)/shard_map/ppermute | solution.py:587
  5.9 7.7 %collective-permute-start.5 = (f32[112,256]{1,0:T(8,128)S(1)}, f32[112,256]{1,0:T(8,128)S(1)}, u32[]{:S(2)}, u32[]{:S(2)}) collective-permute-start(f32[112,256]{1,0:T(8,128)S(1)} %get-tuple-element.44), channel_id=1, source_target_pairs={{0,16},{1,2},{2,1},{3,4},{4,3},{5,6},{6,5},{7,8},{8,7},{9,10},{10,... | collective-permute-start | bytes 344072 | tf_op jit(solution)/shard_map/ppermute | solution.py:588
  9.6 5.7 %collective-permute-start.6 = (f32[184,256]{1,0:T(8,128)S(1)}, f32[184,256]{1,0:T(8,128)S(1)}, u32[]{:S(2)}, u32[]{:S(2)}) collective-permute-start(f32[184,256]{1,0:T(8,128)S(1)} %collective-permute-done.first_ref.gate_ref), channel_id=1, source_target_pairs={{0,16},{1,2},{2,1},{3,19},{4,20},{5,6},{6,5},{7,23},{8,24},{9,10},... | collective-permute-start | bytes 565256 | tf_op jit(solution)/shard_map/ppermute | solution.py:591
  11.7 3.6 %collective-permute-start.3 = (f32[288,256]{1,0:T(8,128)S(1)}, f32[288,256]{1,0:T(8,128)S(1)}, u32[]{:S(2)}, u32[]{:S(2)}) collective-permute-start(f32[288,256]{1,0:T(8,128)S(1)} %release.1), channel_id=1, source_target_pairs={{0,1},{1,0},{2,3},{3,2},{4,5},{5,4},{6,7},{7,6},{8,9},{9,8},{10,11... | collective-permute-start | bytes 884744 | tf_op jit(solution)/shard_map/ppermute | solution.py:590
  11.9 3.4 %collective-permute-start.4 = (f32[296,256]{1,0:T(8,128)S(1)}, f32[296,256]{1,0:T(8,128)S(1)}, u32[]{:S(2)}, u32[]{:S(2)}) collective-permute-start(f32[296,256]{1,0:T(8,128)S(1)} %get-tuple-element.42), channel_id=1, source_target_pairs={{0,1},{1,0},{2,3},{3,2},{4,5},{5,4},{6,7},{7,6},{8,9},{9,8},{10,11... | collective-permute-start | bytes 909320 | tf_op jit(solution)/shard_map/ppermute | solution.py:608
